TPU v7x, 32 devices: a whole 2x2x4 slice. The times are simulated.
32 devices in a mesh: grp: 4 (over x, core), dev: 8 (over z, y).
Axes of the slice: x: 2, y: 2, z: 4, core: 2. Of those that a mesh axis runs over, the one named last changes fastest.
Arguments:
- matrix_slab: float32 [32, 131072], P(None, ('grp', 'dev')), may hold values from -6 to 6
- sign_flips: int32 [131072], P(('grp', 'dev')), may hold values from 0 to 1
- sample_offset: int32 [512], P(('grp', 'dev')), may hold values from 0 to 4095, as said below
Outputs:
- transformed: float32 [32, 131072], P(None, ('grp', 'dev'))
- sketch: float32 [32, 512], P(None, ('grp', 'dev'))
- gram_matrix: float32 [32, 32], replicated
Inputs may be any that keep to these rules, and one draw needn't show every extreme that they name: Entry k selects row (k // 16) * 4096 + sample_offset[k] of the transform; rows may repeat.
All inputs are finite; a program needn't handle non-finite values.
Results may differ from a plain program's by a relative error of at most 0.00011.
Values sent between devices are 32-bit elements; how exact they have to be, the bound alone decides.
No kernel may reach another device: no remote copies, remote signals or barrier semaphores. Data moves between devices by JAX's collectives and lax.ppermute only.
A program may use at most 64 MiB of HBM per device.

v0:
```python
import math

import jax
import jax.numpy as jnp
from jax import lax
from jax.sharding import PartitionSpec as P


def partner_2(block, axis, distance):
    count = lax.axis_size(axis)
    route = []
    for low in range(count):
        high = low | 1 << distance
        if high != low and high < count:
            route += [(low, high), (high, low)]
    return lax.ppermute(block, axis, route)


def hadamard_table(order):
    numbers = jnp.arange(order, dtype=jnp.int32)
    common_bits = numbers[:, None] & numbers[None, :]
    parity = jnp.zeros((order, order), dtype=jnp.int32)
    for position in range(max(order.bit_length() - 1, 0)):
        parity = parity + (common_bits >> position & 1)
    return (1 - 2 * (parity % 2)).astype(jnp.float32)


def mix_local(values):
    columns = values.shape[0]
    local_rows = values.shape[1]
    outer = local_rows // 128
    shaped = values.reshape(columns, outer, 128)
    shaped = jnp.einsum("cak,zk->caz", shaped, hadamard_table(128), precision=lax.Precision.HIGHEST)
    shaped = jnp.einsum(
        "cak,za->czk", shaped, hadamard_table(outer), precision=lax.Precision.HIGHEST
    )
    return shaped


def local(matrix_slab, sign_flips, sample_offset):
    columns = matrix_slab.shape[0]
    local_rows = matrix_slab.shape[1]
    group_count = lax.axis_size("grp")
    dev_count = lax.axis_size("dev")
    total_rows = local_rows * group_count * dev_count
    scaling = jnp.float32(1.0 / math.sqrt(total_rows))
    signs = (1 - 2 * sign_flips).astype(jnp.float32)
    current = mix_local(matrix_slab * signs[None, :])
    dev_place = lax.axis_index("dev")
    for bit_number in range(dev_count.bit_length() - 1):
        partner = partner_2(current, "dev", bit_number)
        lower_side = dev_place >> bit_number & 1 == 0
        current = jnp.where(lower_side, current + partner, partner - current)
    grp_place = lax.axis_index("grp")
    for bit_number in range(group_count.bit_length() - 1):
        partner = partner_2(current, "grp", bit_number)
        lower_side = grp_place >> bit_number & 1 == 0
        current = jnp.where(lower_side, current + partner, partner - current)
    transformed = (current * scaling).reshape(columns, local_rows)
    sketch = jnp.take(transformed, sample_offset, axis=1)
    gram_local = jnp.dot(
        sketch, sketch.T, precision=lax.Precision.HIGHEST, preferred_element_type=jnp.float32
    )
    gram_total = lax.psum(gram_local, ("grp", "dev"))
    sample_total = sample_offset.shape[0] * group_count * dev_count
    gram_matrix = gram_total / jnp.float32(sample_total)
    return (transformed, sketch, gram_matrix)


def solution(mesh):
    return jax.shard_map(
        local,
        mesh=mesh,
        in_specs=(P(None, ("grp", "dev")), P(("grp", "dev")), P(("grp", "dev"))),
        out_specs=(P(None, ("grp", "dev")), P(None, ("grp", "dev")), P()),
        check_vma=False,
    )
```

profile of v0, /device:TPU:0, one launch (start us, length us, event | category | flops | bytes accessed | tf_op | source)
XLA Modules:
  0.0 115.3 jit_solution(3727710240503803801)
XLA Ops:
  0.6 0.7 subtract_convert_fusion
  1.4 1.1 multiply_bitcast_fusion
  2.4 0.1 copy.7
  2.5 0.6 fusion.5
  3.2 0.6 convolution_bitcast_fusion
  3.8 3.0 %collective-permute-start = (f32[32,32,128]{2,1,0:T(8,128)S(1)}, f32[32,32,128]{2,1,0:T(8,128)S(1)}, u32[]{:S(2)}, u32[]{:S(2)}) collective-permute-start(f32[32,32,128]{2,1,0:T(8,128)S(1)} %convolution_bitcast_fusion), channel_id=1, source_target_pairs={{0,1},{1,0},{2,3},{3,2},{4,5},{5,4},{6,7},{7,6},{8,9},{9,8},{10,11... | collective-permute-start | bytes 1572872 | tf_op jit(solution)/shard_map/ppermute | solution.py:16
  6.8 11.9 %collective-permute-done = f32[32,32,128]{2,1,0:T(8,128)S(1)} collective-permute-done((f32[32,32,128]{2,1,0:T(8,128)S(1)}, f32[32,32,128]{2,1,0:T(8,128)S(1)}, u32[]{:S(2)}, u32[]{:S(2)}) %collective-permute-start) | collective-permute-done | bytes 524320 | tf_op jit(solution)/shard_map/ppermute | solution.py:16
  18.8 1.9 %collective-permute-start.1 = (f32[32,32,128]{2,1,0:T(8,128)S(1)}, f32[32,32,128]{2,1,0:T(8,128)S(1)}, u32[]{:S(2)}, u32[]{:S(2)}) collective-permute-start(f32[32,32,128]{2,1,0:T(8,128)S(1)} %subtract_select_fusion.3), channel_id=1, source_target_pairs={{0,2},{2,0},{1,3},{3,1},{4,6},{6,4},{5,7},{7,5},{8,10},{10,8},{9,1... | collective-permute-start | bytes 1572872 | tf_op jit(solution)/shard_map/ppermute | solution.py:16
  20.7 11.3 %collective-permute-done.1 = f32[32,32,128]{2,1,0:T(8,128)S(1)} collective-permute-done((f32[32,32,128]{2,1,0:T(8,128)S(1)}, f32[32,32,128]{2,1,0:T(8,128)S(1)}, u32[]{:S(2)}, u32[]{:S(2)}) %collective-permute-start.1) | collective-permute-done | bytes 524320 | tf_op jit(solution)/shard_map/ppermute | solution.py:16
  32.0 0.1 subtract_select_fusion.2
  32.1 2.6 %collective-permute-start.2 = (f32[32,32,128]{2,1,0:T(8,128)S(1)}, f32[32,32,128]{2,1,0:T(8,128)S(1)}, u32[]{:S(2)}, u32[]{:S(2)}) collective-permute-start(f32[32,32,128]{2,1,0:T(8,128)S(1)} %subtract_select_fusion.2), channel_id=1, source_target_pairs={{0,4},{4,0},{1,5},{5,1},{2,6},{6,2},{3,7},{7,3},{8,12},{12,8},{9,1... | collective-permute-start | bytes 1572872 | tf_op jit(solution)/shard_map/ppermute | solution.py:16
  34.7 21.8 %collective-permute-done.2 = f32[32,32,128]{2,1,0:T(8,128)S(1)} collective-permute-done((f32[32,32,128]{2,1,0:T(8,128)S(1)}, f32[32,32,128]{2,1,0:T(8,128)S(1)}, u32[]{:S(2)}, u32[]{:S(2)}) %collective-permute-start.2) | collective-permute-done | bytes 524320 | tf_op jit(solution)/shard_map/ppermute | solution.py:16
  56.5 0.1 subtract_select_fusion.1
  56.7 1.9 %collective-permute-done.3 = f32[32,32,128]{2,1,0:T(8,128)S(1)} collective-permute-done((f32[32,32,128]{2,1,0:T(8,128)S(1)}, f32[32,32,128]{2,1,0:T(8,128)S(1)}, u32[]{:S(2)}, u32[]{:S(2)}) %collective-permute-start.3) | collective-permute-done | bytes 524320 | tf_op jit(solution)/shard_map/ppermute | solution.py:16
  58.7 1.1 collective-permute-start.4
  59.8 12.9 %collective-permute-done.4 = f32[32,32,128]{2,1,0:T(8,128)S(1)} collective-permute-done((f32[32,32,128]{2,1,0:T(8,128)S(1)}, f32[32,32,128]{2,1,0:T(8,128)S(1)}, u32[]{:S(2)}, u32[]{:S(2)}) %collective-permute-start.4) | collective-permute-done | bytes 524320 | tf_op jit(solution)/shard_map/ppermute | solution.py:16
  72.7 0.1 select_multiply_fusion
  72.8 0.3 copy.10
  73.1 0.6 copy.6
  73.7 0.6 gather_fusion
  74.3 0.3 fusion.31
  74.6 0.7 select_bitcast_fusion
  75.3 39.4 %psum.7 = f32[32,32]{1,0:T(8,128)S(1)} all-reduce(f32[32,32]{1,0:T(8,128)S(1)} %fusion.31), channel_id=1, replica_groups=mesh['grp'=4,'dev'=8] {'grp','dev'}, use_global_device_ids=true, to_apply=%region_0.1 | all-reduce | flops 1024 | bytes 8192 | tf_op jit(solution)/shard_map/psum | solution.py:64
  114.7 0.6 broadcast_multiply_fusion
  (10 shorter events, 0.3 us)
Async XLA Ops:
  3.8 15.0 %collective-permute-start = (f32[32,32,128]{2,1,0:T(8,128)S(1)}, f32[32,32,128]{2,1,0:T(8,128)S(1)}, u32[]{:S(2)}, u32[]{:S(2)}) collective-permute-start(f32[32,32,128]{2,1,0:T(8,128)S(1)} %convolution_bitcast_fusion), channel_id=1, source_target_pairs={{0,1},{1,0},{2,3},{3,2},{4,5},{5,4},{6,7},{7,6},{8,9},{9,8},{10,11... | collective-permute-start | bytes 1572872 | tf_op jit(solution)/shard_map/ppermute | solution.py:16
  18.8 13.2 %collective-permute-start.1 = (f32[32,32,128]{2,1,0:T(8,128)S(1)}, f32[32,32,128]{2,1,0:T(8,128)S(1)}, u32[]{:S(2)}, u32[]{:S(2)}) collective-permute-start(f32[32,32,128]{2,1,0:T(8,128)S(1)} %subtract_select_fusion.3), channel_id=1, source_target_pairs={{0,2},{2,0},{1,3},{3,1},{4,6},{6,4},{5,7},{7,5},{8,10},{10,8},{9,1... | collective-permute-start | bytes 1572872 | tf_op jit(solution)/shard_map/ppermute | solution.py:16
  20.7 39.1 %copy-start.1 = (s32[16]{0:T(128)S(1)}, s32[16]{0:T(128)}, u32[]{:S(2)}) copy-start(s32[16]{0:T(128)} %param.5) | copy-start | bytes 196
  32.1 24.4 %collective-permute-start.2 = (f32[32,32,128]{2,1,0:T(8,128)S(1)}, f32[32,32,128]{2,1,0:T(8,128)S(1)}, u32[]{:S(2)}, u32[]{:S(2)}) collective-permute-start(f32[32,32,128]{2,1,0:T(8,128)S(1)} %subtract_select_fusion.2), channel_id=1, source_target_pairs={{0,4},{4,0},{1,5},{5,1},{2,6},{6,2},{3,7},{7,3},{8,12},{12,8},{9,1... | collective-permute-start | bytes 1572872 | tf_op jit(solution)/shard_map/ppermute | solution.py:16
  56.6 2.0 %collective-permute-start.3 = (f32[32,32,128]{2,1,0:T(8,128)S(1)}, f32[32,32,128]{2,1,0:T(8,128)S(1)}, u32[]{:S(2)}, u32[]{:S(2)}) collective-permute-start(f32[32,32,128]{2,1,0:T(8,128)S(1)} %subtract_select_fusion.1), channel_id=1, source_target_pairs={{0,8},{8,0},{16,24},{24,16},{1,9},{9,1},{17,25},{25,17},{2,10},{10... | collective-permute-start | bytes 1572872 | tf_op jit(solution)/shard_map/ppermute | solution.py:16
  58.7 14.0 %collective-permute-start.4 = (f32[32,32,128]{2,1,0:T(8,128)S(1)}, f32[32,32,128]{2,1,0:T(8,128)S(1)}, u32[]{:S(2)}, u32[]{:S(2)}) collective-permute-start(f32[32,32,128]{2,1,0:T(8,128)S(1)} %subtract_select_fusion), channel_id=1, source_target_pairs={{0,16},{16,0},{8,24},{24,8},{1,17},{17,1},{9,25},{25,9},{2,18},{18... | collective-permute-start | bytes 1572872 | tf_op jit(solution)/shard_map/ppermute | solution.py:16
  73.1 42.2 %copy-start = (f32[4,8,32,128]{3,1,2,0:T(8,128)}, f32[4,8,32,128]{3,1,2,0:T(8,128)S(1)}, u32[]{:S(2)}) copy-start(f32[4,8,32,128]{3,1,2,0:T(8,128)S(1)} %copy.10) | copy-start | bytes 1572868
where the time goes:
time: 116 us; the launch traced here: 115 us
  waiting for transfers between devices  59.8 us (52%)
  blocking collectives  39.4 us (34%)
  starting transfers between devices  8.67 us (7%)
  other arithmetic  3.59 us (3%)
  local copies, waits for them, and re-layouts  1.58 us (1%)
  matrix products  1.5 us (1%)
    ppermute x5, waiting for transfers between devices, partner_2(): return lax.ppermute(block, axis, route)  59.8 us
    psum x1, blocking collectives, local(): gram_total = lax.psum(gram_local, ('grp', 'dev'))  39.4 us
    ppermute x5, starting transfers between devices, partner_2(): return lax.ppermute(block, axis, route)  8.67 us
  transfers between devices with their start and end apart: 5, of which 5 were waited for; matrix products, arithmetic and copies ran while one was open for 0% of the time, Pallas kernels for 0%

commit v1 on v0

v1 whole, which is shorter than its diff:
```python
import functools
import math

import jax
import jax.numpy as jnp
from jax import lax
from jax.experimental import pallas as pl
from jax.experimental.pallas import tpu as pltpu
from jax.sharding import PartitionSpec as P

AXES = ("grp", "dev")
LANES = 128
ROWS = 8
IN_VMEM = pl.BlockSpec(memory_space=pltpu.VMEM)
IN_SMEM = pl.BlockSpec(memory_space=pltpu.SMEM)
IN_HBM = pl.BlockSpec(memory_space=pltpu.HBM)


def call(body, outputs, in_specs, args, out_specs=None, scratch=()):
    return pl.pallas_call(
        body,
        out_shape=outputs,
        in_specs=in_specs,
        out_specs=jax.tree.map(lambda _: IN_VMEM, outputs) if out_specs is None else out_specs,
        scratch_shapes=scratch,
        compiler_params=pltpu.CompilerParams(vmem_limit_bytes=24 * 1024 * 1024),
    )(*args)


def block(rows, width, dtype=jnp.float32):
    return jax.ShapeDtypeStruct((rows, width), dtype)


def lanes_of(index):
    return slice(index * LANES, (index + 1) * LANES)


def exchange(array, core, masks):
    count = lax.axis_size(AXES)
    route = [(place, place ^ masks[0 if place & core == 0 else 1]) for place in range(count)]
    return lax.ppermute(array, AXES, route)


def chosen_mask(place, core, masks):
    return jnp.where(place & core == 0, masks[0], masks[1])


def combine(current, partner, core, masks):
    place = lax.axis_index(AXES)
    lower = place & chosen_mask(place, core, masks) == 0
    return jnp.where(lower, current + partner, partner - current)


def three_parts(values):
    high = values.astype(jnp.bfloat16)
    rest = values - high.astype(jnp.float32)
    middle = rest.astype(jnp.bfloat16)
    low = (rest - middle.astype(jnp.float32)).astype(jnp.bfloat16)
    return high, middle, low


def exact_dot(values, table):
    total = None
    for piece in three_parts(values):
        product = jnp.dot(piece, table, preferred_element_type=jnp.float32)
        total = product if total is None else total + product
    return total


def mix(parts):
    left = lax.broadcasted_iota(jnp.int32, (LANES, LANES), 0)
    right = lax.broadcasted_iota(jnp.int32, (LANES, LANES), 1)
    parity = left & right
    for shift in (4, 2, 1):
        parity = parity ^ (parity >> shift)
    table = (1 - 2 * (parity & 1)).astype(jnp.float32).astype(jnp.bfloat16)
    parts = list(parts)
    span = 1
    while span < len(parts):
        for index in range(len(parts)):
            if index & span == 0:
                first, second = parts[index], parts[index | span]
                parts[index], parts[index | span] = first + second, first - second
        span *= 2
    total = exact_dot(jnp.concatenate(parts, axis=0), table)
    rows = parts[0].shape[0]
    return [total[index * rows : (index + 1) * rows] for index in range(len(parts))]


def own_kernel(scaling, core, place_ref, slab_ref, flips_ref, out_ref):
    columns = out_ref.shape[0]
    top = jnp.where(place_ref[0] & core == 0, 0, columns)
    for index in range(flips_ref.shape[0]):
        sign = jnp.where(flips_ref[index : index + 1, :] == 0, scaling, -scaling)
        rows = pl.ds(pl.multiple_of(top, ROWS), columns)
        out_ref[:, lanes_of(index)] = slab_ref[rows, lanes_of(index)] * sign


def split_kernel(scaling, core, place_ref, own_ref, other_ref, flips_ref, offset_ref, other_offset_ref, *out_refs):
    chunk_refs, tile_ref = out_refs[:-1], out_refs[-1]
    columns = own_ref.shape[0]
    on_first = place_ref[0] & core == 0
    top = jnp.where(on_first, 0, columns)
    turn = jnp.where(on_first, 1.0, -1.0)
    for index in range(flips_ref.shape[0]):
        here = lanes_of(index)
        sign = jnp.where(flips_ref[index : index + 1, :] == 0, scaling, -scaling)
        for number, chunk_ref in enumerate(chunk_refs):
            own = own_ref[number * ROWS : (number + 1) * ROWS, here]
            other = other_ref[pl.ds(pl.multiple_of(top + number * ROWS, ROWS), ROWS), here] * sign
            chunk_ref[:ROWS, here] = own + other
            chunk_ref[ROWS:, here] = (own - other) * turn
    samples = offset_ref.shape[1]
    first = jnp.where(on_first, offset_ref[...], other_offset_ref[...])
    second = jnp.where(on_first, other_offset_ref[...], offset_ref[...])
    tile = jnp.concatenate([first, second] * (LANES // (2 * samples)), axis=1)
    tile_ref[...] = jnp.broadcast_to(tile.astype(jnp.float32), tile_ref.shape)


def mix_kernel(core, masks, place_ref, own_ref, other_ref, tile_ref, out_ref):
    slices = own_ref.shape[1] // LANES
    factor = jnp.where(place_ref[0] & chosen_mask(place_ref[0], core, masks) == 0, 1.0, -1.0)
    parts = [
        own_ref[:, lanes_of(index)] * factor + other_ref[:, lanes_of(index)] for index in range(slices)
    ]
    for index, part in enumerate(mix(parts)):
        out_ref[:, lanes_of(index)] = part
    for row in range(0, own_ref.shape[0], ROWS):
        out_ref[row : row + ROWS, lanes_of(slices)] = tile_ref[...]


def second_kernel(core, masks, place_ref, own_ref, other_ref, out_ref):
    factor = jnp.where(place_ref[0] & chosen_mask(place_ref[0], core, masks) == 0, 1.0, -1.0)
    width = out_ref.shape[1]
    out_ref[...] = own_ref[:, :width] * factor + other_ref[:, :width]


def pick_kernel(core, all_masks, place_ref, tile_ref, *refs):
    count = len(all_masks)
    chunk_refs, other_refs, out_ref = refs[:count], refs[count:-1], refs[-1]
    samples = out_ref.shape[1] * 2
    lane = lax.broadcasted_iota(jnp.int32, (1, LANES), 1)
    place_in = lax.broadcasted_iota(jnp.int32, (LANES, LANES), 0)
    own_chip = lane < 2 * samples
    shares = []
    for masks, chunk_ref, other_ref in zip(all_masks, chunk_refs, other_refs):
        partner = other_ref[0:1, other_ref.shape[1] - LANES :]
        offsets = jnp.where(own_chip, tile_ref[0:1, :], partner).astype(jnp.int32)
        chosen = jnp.where(place_in == offsets % LANES, 1.0, 0.0).astype(jnp.bfloat16)
        side = jnp.where(place_ref[0] & chosen_mask(place_ref[0], core, masks) == 0, 1.0, -1.0)
        slices = chunk_ref.shape[1] // LANES
        rows = chunk_ref.shape[0]
        stacked = jnp.concatenate([chunk_ref[:, lanes_of(index)] for index in range(slices)], axis=0)
        found = exact_dot(stacked, chosen)
        share = jnp.zeros((rows, LANES), jnp.float32)
        for index in range(slices):
            share = jnp.where(offsets // LANES == index, found[index * rows : (index + 1) * rows], share)
        share = jnp.where(lane // samples % 2 == 0, share[:ROWS], share[ROWS:])
        shares.append(share * jnp.where(own_chip, side, 1.0))
    turned = jnp.concatenate(shares, axis=0).T
    half = samples // 2
    starts = [kind * samples + part * half for part in range(2) for kind in range(4)]
    tile = jnp.concatenate([turned[start : start + half] for start in starts], axis=1)
    for place in range(out_ref.shape[0]):
        out_ref[place] = tile


def gram_kernel(core, all_masks, place_ref, shares_ref, gram_ref, sketch_ref):
    count, rows, _ = shares_ref.shape
    columns = gram_ref.shape[0]
    width = columns // 2
    lane = lax.broadcasted_iota(jnp.int32, (rows, LANES), 1)
    number = lane % width // ROWS

    def of_core(place, second):
        others = shares_ref[place ^ all_masks[0][second]]
        for chunk in range(1, len(all_masks)):
            others = jnp.where(number == chunk, shares_ref[place ^ all_masks[chunk][second]], others)
        return shares_ref[place] + pltpu.roll(others, LANES - columns, 1)

    def of_chip(place):
        second = pltpu.roll(of_core(place | core, 1), columns, 1)
        return jnp.where(lane % (2 * columns) < columns, of_core(place, 0), second)

    chips = [place for place in range(count) if place & core == 0]
    stacked = jnp.concatenate([of_chip(place) for place in chips], axis=0)
    product = functools.partial(
        lax.dot_general, precision=lax.Precision.HIGHEST, preferred_element_type=jnp.float32
    )
    gram = product(stacked, stacked, (((0,), (0,)), ((), ())))
    down = lax.broadcasted_iota(jnp.int32, (LANES, LANES), 0)
    across = lax.broadcasted_iota(jnp.int32, (LANES, LANES), 1)

    def sample_of(spot):
        return spot // (2 * columns) * 2 + spot // width % 2

    gram = jnp.where(sample_of(down) == sample_of(across), gram, 0.0)
    spot = lax.broadcasted_iota(jnp.int32, (LANES, columns), 0)
    column = lax.broadcasted_iota(jnp.int32, (LANES, columns), 1)
    column_of = spot // columns % 2 * width + spot % width
    fold = jnp.where(column_of == column, 1.0, 0.0)
    gram = product(product(gram, fold, (((1,), (0,)), ((), ()))), fold, (((0,), (0,)), ((), ())))
    gram_ref[...] = gram * (1.0 / (count * 2 * rows))
    chip = place_ref[0] & ~core
    own = of_chip(chip)
    on_second = jnp.where(place_ref[0] & core == 0, 0, 1)
    for part in range(2):
        wanted = (column_of == column) & (sample_of(spot) == part * 2 + on_second)
        sketch_ref[part * rows : (part + 1) * rows] = exact_dot(
            own, jnp.where(wanted, 1.0, 0.0).astype(jnp.bfloat16)
        )


def last_kernel(core, masks, place_ref, own_ref, other_ref, keep_ref, send_ref):
    on_first = place_ref[0] & core == 0
    factor = jnp.where(place_ref[0] & chosen_mask(place_ref[0], core, masks) == 0, 1.0, -1.0)
    for out_ref, top in ((keep_ref, jnp.where(on_first, 0, ROWS)), (send_ref, jnp.where(on_first, ROWS, 0))):
        rows = pl.ds(pl.multiple_of(top, ROWS), ROWS)
        out_ref[...] = own_ref[rows, :] * factor + other_ref[rows, :]


def join_kernel(core, place_ref, *refs):
    block_refs, (whole_ref, sems) = refs[:-2], refs[-2:]
    on_first = place_ref[0] & core == 0
    half = whole_ref.shape[0] // 2
    tops = []
    for kept in (True, False):
        base = jnp.where(on_first, 0, half) if kept else jnp.where(on_first, half, 0)
        tops += [base + row for row in range(0, half, ROWS)]
    copies = [
        pltpu.make_async_copy(
            block_ref, whole_ref.at[pl.ds(pl.multiple_of(top, ROWS), ROWS)], sems.at[number]
        )
        for number, (block_ref, top) in enumerate(zip(block_refs, tops))
    ]
    for copy in copies:
        copy.start()
    for copy in copies:
        copy.wait()


def local_any(matrix_slab, sign_flips, sample_offset):
    columns, local_rows = matrix_slab.shape
    count = lax.axis_size(AXES)
    samples = sample_offset.shape[0]
    numbers = jnp.arange(local_rows, dtype=jnp.int32)

    def table(order):
        common = numbers[:order, None] & numbers[None, :order]
        return (1 - 2 * (lax.population_count(common) & 1)).astype(jnp.float32)

    signs = (1 - 2 * sign_flips).astype(jnp.float32) * jnp.float32(1.0 / math.sqrt(local_rows * count))
    outer = local_rows // LANES
    shaped = (matrix_slab * signs[None, :]).reshape(columns, outer, LANES)
    shaped = jnp.einsum("cak,kz->caz", shaped, table(LANES), precision=lax.Precision.HIGHEST)
    shaped = jnp.einsum("cak,az->czk", shaped, table(outer), precision=lax.Precision.HIGHEST)
    current = shaped.reshape(columns, local_rows)
    for bit in range(count.bit_length() - 1):
        masks = (1 << bit, 1 << bit)
        current = combine(current, exchange(current, 1, masks), 1, masks)
    sketch = jnp.take(current, sample_offset, axis=1)
    gram = jnp.dot(sketch, sketch.T, precision=lax.Precision.HIGHEST)
    return (current, sketch, lax.psum(gram, AXES) / jnp.float32(samples * count))


def local(matrix_slab, sign_flips, sample_offset):
    columns, local_rows = matrix_slab.shape
    grp_bits = lax.axis_size("grp").bit_length() - 1
    dev_bits = lax.axis_size("dev").bit_length() - 1
    count = lax.axis_size(AXES)
    samples = sample_offset.shape[0]
    if (grp_bits, dev_bits, columns, samples) != (2, 3, 4 * ROWS, 2 * ROWS):
        return local_any(matrix_slab, sign_flips, sample_offset)
    place = lax.axis_index(AXES).astype(jnp.int32).reshape(1)
    flips = sign_flips.reshape(local_rows // LANES, LANES)
    offsets = sample_offset.reshape(1, samples)
    y, z_low, z_high, core, x = (1 << bit for bit in range(dev_bits + grp_bits))
    scaling = 1.0 / math.sqrt(local_rows * count)
    across = (core, core)
    orders = [
        [(y, z_low), (z_low, y), (x, z_high), (z_high, x)],
        [(x, z_high), (z_high, x), (y, z_low), (z_low, y)],
    ]

    other = exchange(matrix_slab, core, across)
    other_flips = exchange(flips, core, across)
    other_offsets = exchange(offsets, core, across)
    own = call(
        functools.partial(own_kernel, scaling, core),
        block(columns // 2, local_rows),
        [IN_SMEM, IN_VMEM, IN_VMEM],
        [place, matrix_slab, flips],
    )
    chunk = block(2 * ROWS, local_rows)
    *chunks, tile = call(
        functools.partial(split_kernel, scaling, core),
        [chunk, chunk, block(ROWS, LANES)],
        [IN_SMEM] + [IN_VMEM] * 5,
        [place, own, other, other_flips, offsets, other_offsets],
    )
    almost, ridden, lasts = [], [], []
    for current, order in zip(chunks, orders):
        partner = exchange(current, core, order[0])
        current = call(
            functools.partial(mix_kernel, core, order[0]),
            block(2 * ROWS, local_rows + LANES),
            [IN_SMEM] + [IN_VMEM] * 3,
            [place, current, partner, tile],
        )
        partner = exchange(current, core, order[1])
        ridden.append(partner)
        current = call(
            functools.partial(second_kernel, core, order[1]),
            chunk,
            [IN_SMEM] + [IN_VMEM] * 2,
            [place, current, partner],
        )
        current = combine(current, exchange(current, core, order[2]), core, order[2])
        almost.append(current)
        lasts.append(
            call(
                functools.partial(last_kernel, core, order[3]),
                [block(ROWS, local_rows)] * 2,
                [IN_SMEM] + [IN_VMEM] * 2,
                [place, current, exchange(current, core, order[3])],
            )
        )
    last_masks = [order[3] for order in orders]
    shares = call(
        functools.partial(pick_kernel, core, last_masks),
        jax.ShapeDtypeStruct((count, samples // 2, LANES), jnp.float32),
        [IN_SMEM] + [IN_VMEM] * 5,
        [place, tile, *almost, *ridden[::-1]],
    )
    gram, sketch = call(
        functools.partial(gram_kernel, core, last_masks),
        [block(columns, columns), block(samples, columns)],
        [IN_SMEM, IN_VMEM],
        [place, lax.all_to_all(shares, AXES, 0, 0, tiled=True)],
    )
    kept = [keep for keep, _ in lasts]
    back = [exchange(send, core, across) for _, send in lasts]
    transformed = call(
        functools.partial(join_kernel, core),
        block(columns, local_rows),
        [IN_SMEM] + [IN_VMEM] * 4,
        [place, *kept, *back],
        out_specs=IN_HBM,
        scratch=[pltpu.SemaphoreType.DMA((4,))],
    )
    return (transformed, sketch.T, gram)


def solution(mesh):
    return jax.shard_map(
        local,
        mesh=mesh,
        in_specs=(P(None, AXES), P(AXES), P(AXES)),
        out_specs=(P(None, AXES), P(None, AXES), P()),
        check_vma=False,
    )
```

time: 116 us -> 47.5 us (0.41)
  waiting for transfers between devices: 59.8 us -> 19.6 us
  blocking collectives: 39.4 us -> 0 us
  starting transfers between devices: 8.67 us -> 21 us
  Pallas kernels: 0 us -> 4.42 us
  other arithmetic: 3.59 us -> 0.06 us
  matrix products: 1.5 us -> 0 us
    ppermute x5 -> x13, waiting for transfers between devices: 59.8 us -> 14.9 us  [exchange(): return lax.ppermute(array, AXES, route)]
    psum x1 -> x0, blocking collectives: 39.4 us -> none  [local(): gram_total = lax.psum(gram_local, ('grp', 'dev'))]
    ppermute x5 -> x13, starting transfers between devices: 8.67 us -> 17.5 us  [exchange(): return lax.ppermute(array, AXES, route)]
    all_to_all x0 -> x1, waiting for transfers between devices: none -> 4.75 us  [local(): lax.all_to_all(shares, AXES, 0, 0, tiled=True)]
    pallas_call x0 -> x11, Pallas kernels: none -> 4.42 us  [call(): pl.pallas_call(body, out_shape=outputs, in_specs=in_specs, out_specs=jax....]
    all_to_all x0 -> x1, starting transfers between devices: none -> 3.49 us  [local(): lax.all_to_all(shares, AXES, 0, 0, tiled=True)]
    dot_general x3 -> x0, matrix products: 1.5 us -> none  [the longest x1 0.64 us: mix_local(): jnp.einsum('cak,zk->caz', shaped, hadamard_table(128), precision=lax.Prec...]
  transfers between devices with their start and end apart: 5 -> 14, of which waited for: 5 -> 7; matrix products, arithmetic and copies ran while one was open for 0% -> 0% of each run, Pallas kernels for 0% -> 7%
where the time goes in v1:
time: 47.5 us; the launch traced here: 47.2 us
  starting transfers between devices  21 us (44%)
  waiting for transfers between devices  19.6 us (41%)
  Pallas kernels  4.42 us (9%)
  local copies, waits for them, and re-layouts  1.48 us (3%)
  between operations  0.72 us (2%)
    ppermute x13, starting transfers between devices, exchange(): return lax.ppermute(array, AXES, route)  17.5 us
    ppermute x13, waiting for transfers between devices, exchange(): return lax.ppermute(array, AXES, route)  14.9 us
    all_to_all x1, waiting for transfers between devices, local(): lax.all_to_all(shares, AXES, 0, 0, tiled=True)  4.75 us
    pallas_call x11, Pallas kernels, call(): pl.pallas_call(body, out_shape=outputs, in_specs=in_specs, out_specs=jax....  4.42 us
    all_to_all x1, starting transfers between devices, local(): lax.all_to_all(shares, AXES, 0, 0, tiled=True)  3.49 us
    unnamed x6, local copies, waits for them, and re-layouts  1.48 us
  transfers between devices with their start and end apart: 14, of which 7 were waited for; matrix products, arithmetic and copies ran while one was open for 0% of the time, Pallas kernels for 7%

profile of v1, /device:TPU:0, one launch (start us, length us, event | category | flops | bytes accessed | tf_op | source)
XLA Modules:
  0.0 47.2 jit_solution(16836710831401375248)
XLA Ops:
  0.6 0.5 %collective-permute-start = (f32[32,4096]{1,0:T(8,128)}, f32[32,4096]{1,0:T(8,128)S(1)}, u32[]{:S(2)}, u32[]{:S(2)}) collective-permute-start(f32[32,4096]{1,0:T(8,128)} %slab_ref.1), channel_id=1, source_target_pairs={{0,8},{1,9},{2,10},{3,11},{4,12},{5,13},{6,14},{7,15},{8,0},{9,1},... | collective-permute-start | bytes 1572872 | tf_op jit(solution)/shard_map/ppermute | solution.py:41
  1.2 0.4 collective-permute-start.2
  1.7 1.0 %copy-done = f32[32,4096]{1,0:T(8,128)S(1)} copy-done((f32[32,4096]{1,0:T(8,128)S(1)}, f32[32,4096]{1,0:T(8,128)}, u32[]{:S(2)}) %copy-start) | copy-done | bytes 524312
  2.9 0.4 copy-done.2
  3.5 2.7 %collective-permute-start.7 = (f32[16,4096]{1,0:T(8,128)S(1)}, f32[16,4096]{1,0:T(8,128)S(1)}, u32[]{:S(2)}, u32[]{:S(2)}) collective-permute-start(f32[16,4096]{1,0:T(8,128)S(1)} %get-tuple-element.15.own_ref), channel_id=1, source_target_pairs={{0,16},{1,17},{2,18},{3,19},{4,20},{5,21},{6,22},{7,23},{8,12},{9,... | collective-permute-start | bytes 786440 | tf_op jit(solution)/shard_map/ppermute | solution.py:41
  6.1 1.5 %collective-permute-start.3 = (f32[16,4096]{1,0:T(8,128)S(1)}, f32[16,4096]{1,0:T(8,128)S(1)}, u32[]{:S(2)}, u32[]{:S(2)}) collective-permute-start(f32[16,4096]{1,0:T(8,128)S(1)} %get-tuple-element.12.own_ref), channel_id=1, source_target_pairs={{0,1},{1,0},{2,3},{3,2},{4,5},{5,4},{6,7},{7,6},{8,10},{9,11},{10,... | collective-permute-start | bytes 786440 | tf_op jit(solution)/shard_map/ppermute | solution.py:41
  7.6 2.8 %collective-permute-done.7.other_ref = f32[16,4096]{1,0:T(8,128)S(1)} collective-permute-done((f32[16,4096]{1,0:T(8,128)S(1)}, f32[16,4096]{1,0:T(8,128)S(1)}, u32[]{:S(2)}, u32[]{:S(2)}) %collective-permute-start.7) | collective-permute-done | bytes 262176 | tf_op jit(solution)/shard_map/ppermute | solution.py:41
  10.8 3.2 %collective-permute-start.8 = (f32[16,4224]{1,0:T(8,128)S(1)}, f32[16,4224]{1,0:T(8,128)S(1)}, u32[]{:S(2)}, u32[]{:S(2)}) collective-permute-start(f32[16,4224]{1,0:T(8,128)S(1)} %shard_map.63.own_ref), channel_id=1, source_target_pairs={{0,4},{1,5},{2,6},{3,7},{4,0},{5,1},{6,2},{7,3},{8,24},{9,25},{10,... | collective-permute-start | bytes 811016 | tf_op jit(solution)/shard_map/ppermute | solution.py:41
  14.0 0.3 shard_map.60.own_ref
  14.3 1.6 %collective-permute-start.4 = (f32[16,4224]{1,0:T(8,128)S(1)}, f32[16,4224]{1,0:T(8,128)S(1)}, u32[]{:S(2)}, u32[]{:S(2)}) collective-permute-start(f32[16,4224]{1,0:T(8,128)S(1)} %shard_map.60.own_ref), channel_id=1, source_target_pairs={{0,2},{1,3},{2,0},{3,1},{4,6},{5,7},{6,4},{7,5},{8,9},{9,8},{10,11... | collective-permute-start | bytes 811016 | tf_op jit(solution)/shard_map/ppermute | solution.py:41
  15.9 5.5 %collective-permute-done.8.other_ref.refs_2_ = f32[16,4224]{1,0:T(8,128)S(1)} collective-permute-done((f32[16,4224]{1,0:T(8,128)S(1)}, f32[16,4224]{1,0:T(8,128)S(1)}, u32[]{:S(2)}, u32[]{:S(2)}) %collective-permute-start.8) | collective-permute-done | bytes 270368 | tf_op jit(solution)/shard_map/ppermute | solution.py:41
  21.5 1.9 %collective-permute-start.9 = (f32[16,4096]{1,0:T(8,128)S(1)}, f32[16,4096]{1,0:T(8,128)S(1)}, u32[]{:S(2)}, u32[]{:S(2)}) collective-permute-start(f32[16,4096]{1,0:T(8,128)S(1)} %shard_map.64), channel_id=1, source_target_pairs={{0,1},{1,0},{2,3},{3,2},{4,5},{5,4},{6,7},{7,6},{8,10},{9,11},{10,... | collective-permute-start | bytes 786440 | tf_op jit(solution)/shard_map/ppermute | solution.py:41
  23.4 1.6 %collective-permute-start.5 = (f32[16,4096]{1,0:T(8,128)S(1)}, f32[16,4096]{1,0:T(8,128)S(1)}, u32[]{:S(2)}, u32[]{:S(2)}) collective-permute-start(f32[16,4096]{1,0:T(8,128)S(1)} %shard_map.61), channel_id=1, source_target_pairs={{0,16},{1,17},{2,18},{3,19},{4,20},{5,21},{6,22},{7,23},{8,12},{9,... | collective-permute-start | bytes 786440 | tf_op jit(solution)/shard_map/ppermute | solution.py:41
  25.0 2.9 %collective-permute-done.9 = f32[16,4096]{1,0:T(8,128)S(1)} collective-permute-done((f32[16,4096]{1,0:T(8,128)S(1)}, f32[16,4096]{1,0:T(8,128)S(1)}, u32[]{:S(2)}, u32[]{:S(2)}) %collective-permute-start.9) | collective-permute-done | bytes 262176 | tf_op jit(solution)/shard_map/ppermute | solution.py:41
  27.9 1.0 %collective-permute-start.10 = (f32[16,4096]{1,0:T(8,128)S(1)}, f32[16,4096]{1,0:T(8,128)S(1)}, u32[]{:S(2)}, u32[]{:S(2)}) collective-permute-start(f32[16,4096]{1,0:T(8,128)S(1)} %subtract_select_fusion.own_ref.refs_1_), channel_id=1, source_target_pairs={{0,2},{1,3},{2,0},{3,1},{4,6},{5,7},{6,4},{7,5},{8,9},{9,8},{10,11... | collective-permute-start | bytes 786440 | tf_op jit(solution)/shard_map/ppermute | solution.py:41
  28.9 0.9 %collective-permute-done.5 = f32[16,4096]{1,0:T(8,128)S(1)} collective-permute-done((f32[16,4096]{1,0:T(8,128)S(1)}, f32[16,4096]{1,0:T(8,128)S(1)}, u32[]{:S(2)}, u32[]{:S(2)}) %collective-permute-start.5) | collective-permute-done | bytes 262176 | tf_op jit(solution)/shard_map/ppermute | solution.py:41
  29.9 2.6 %collective-permute-start.6 = (f32[16,4096]{1,0:T(8,128)S(1)}, f32[16,4096]{1,0:T(8,128)S(1)}, u32[]{:S(2)}, u32[]{:S(2)}) collective-permute-start(f32[16,4096]{1,0:T(8,128)S(1)} %subtract_select_fusion.1.own_ref.refs_0_), channel_id=1, source_target_pairs={{0,4},{1,5},{2,6},{3,7},{4,0},{5,1},{6,2},{7,3},{8,24},{9,25},{10,... | collective-permute-start | bytes 786440 | tf_op jit(solution)/shard_map/ppermute | solution.py:41
  32.5 1.2 %shard_map.67 = f32[32,8,128]{2,1,0:T(8,128)} custom-call(s32[1]{0:T(128)} %bitcast.place_ref, f32[8,128]{1,0:T(8,128)S(1)} %get-tuple-element.13.tile_ref, f32[16,4096]{1,0:T(8,128)S(1)} %subtract_select_fusion.1.own_ref.refs_0_, f32[16,4096]{1,0:T(8,128)S(1)} %subtract_select_fusion.own_ref.refs_1_, ...), custom_call_target="tpu_custom_call" | custom-call | tf_op jit(solution)/shard_map/pallas_call | solution.py:20
  33.7 3.5 %all-to-all-start = ((f32[32,8,128]{2,1,0:T(8,128)}), f32[32,8,128]{2,1,0:T(8,128)S(1)}, u32[]{:S(2)}, u32[]{:S(2)}) async-start(f32[32,8,128]{2,1,0:T(8,128)} %shard_map.67), calls=%async_computation | async-start | bytes 262144 | tf_op jit(solution)/shard_map/all_to_all | solution.py:339
  37.2 0.3 collective-permute-start.12
  37.5 2.5 %collective-permute-done.6.other_ref = f32[16,4096]{1,0:T(8,128)S(1)} collective-permute-done((f32[16,4096]{1,0:T(8,128)S(1)}, f32[16,4096]{1,0:T(8,128)S(1)}, u32[]{:S(2)}, u32[]{:S(2)}) %collective-permute-start.6) | collective-permute-done | bytes 262176 | tf_op jit(solution)/shard_map/ppermute | solution.py:41
  40.1 4.8 %all-to-all-done.shares_ref = f32[32,8,128]{2,1,0:T(8,128)S(1)} async-done(((f32[32,8,128]{2,1,0:T(8,128)}), f32[32,8,128]{2,1,0:T(8,128)S(1)}, u32[]{:S(2)}, u32[]{:S(2)}) %all-to-all-start) | async-done | bytes 131104 | tf_op jit(solution)/shard_map/all_to_all | solution.py:339
  44.9 1.5 %shard_map.68 = (f32[32,32]{1,0:T(8,128)}, f32[16,32]{1,0:T(8,128)}) custom-call(s32[1]{0:T(128)} %bitcast.place_ref, f32[32,8,128]{2,1,0:T(8,128)S(1)} %all-to-all-done.shares_ref), custom_call_target="tpu_custom_call" | custom-call | tf_op jit(solution)/shard_map/pallas_call | solution.py:20
  46.4 0.8 %shard_map.66 = f32[32,4096]{1,0:T(8,128)} custom-call(s32[1]{0:T(128)} %bitcast.place_ref, f32[8,4096]{1,0:T(8,128)S(1)} %get-tuple-element.14.refs_0_, f32[8,4096]{1,0:T(8,128)S(1)} %get-tuple-element.16.refs_1_, f32[8,4096]{1,0:T(8,128)S(1)} %collective-permute-done.11.refs_2_, f32[8,4096]{1,0:T(8,128)S(1)} %collective-permute-done.12.refs_3_), custom_call_target="tpu_custom_call" | custom-call | tf_op jit(solution)/shard_map/pallas_call | solution.py:20
  (23 shorter events, 1.0 us)
Async XLA Ops:
  0.6 1.0 %copy-start.1 = (s32[4096]{0:T(1024)S(1)}, s32[4096]{0:T(1024)}, u32[]{:S(2)}) copy-start(s32[4096]{0:T(1024)} %param.4) | copy-start | bytes 49156
  0.6 2.3 %collective-permute-start = (f32[32,4096]{1,0:T(8,128)}, f32[32,4096]{1,0:T(8,128)S(1)}, u32[]{:S(2)}, u32[]{:S(2)}) collective-permute-start(f32[32,4096]{1,0:T(8,128)} %slab_ref.1), channel_id=1, source_target_pairs={{0,8},{1,9},{2,10},{3,11},{4,12},{5,13},{6,14},{7,15},{8,0},{9,1},... | collective-permute-start | bytes 1572872 | tf_op jit(solution)/shard_map/ppermute | solution.py:41
  1.2 1.8 %collective-permute-start.1 = (s32[32,128]{1,0:T(8,128)}, s32[32,128]{1,0:T(8,128)S(1)}, u32[]{:S(2)}, u32[]{:S(2)}) collective-permute-start(s32[32,128]{1,0:T(8,128)} %bitcast.4), channel_id=1, source_target_pairs={{0,8},{1,9},{2,10},{3,11},{4,12},{5,13},{6,14},{7,15},{8,0},{9,1},... | collective-permute-start | bytes 49160 | tf_op jit(solution)/shard_map/ppermute | solution.py:41
  1.2 1.7 %collective-permute-start.2 = (s32[1,16]{1,0:T(1,128)}, s32[1,16]{1,0:T(1,128)S(1)}, u32[]{:S(2)}, u32[]{:S(2)}) collective-permute-start(s32[1,16]{1,0:T(1,128)} %bitcast.6), channel_id=1, source_target_pairs={{0,8},{1,9},{2,10},{3,11},{4,12},{5,13},{6,14},{7,15},{8,0},{9,1},... | collective-permute-start | bytes 200 | tf_op jit(solution)/shard_map/ppermute | solution.py:41
  1.7 1.0 %copy-start = (f32[32,4096]{1,0:T(8,128)S(1)}, f32[32,4096]{1,0:T(8,128)}, u32[]{:S(2)}) copy-start(f32[32,4096]{1,0:T(8,128)} %slab_ref.1) | copy-start | bytes 1572868
  2.7 0.7 %copy-start.2 = (s32[16]{0:T(128)S(1)}, s32[16]{0:T(128)}, u32[]{:S(2)}) copy-start(s32[16]{0:T(128)} %param.5) | copy-start | bytes 196
  3.5 7.0 %collective-permute-start.7 = (f32[16,4096]{1,0:T(8,128)S(1)}, f32[16,4096]{1,0:T(8,128)S(1)}, u32[]{:S(2)}, u32[]{:S(2)}) collective-permute-start(f32[16,4096]{1,0:T(8,128)S(1)} %get-tuple-element.15.own_ref), channel_id=1, source_target_pairs={{0,16},{1,17},{2,18},{3,19},{4,20},{5,21},{6,22},{7,23},{8,12},{9,... | collective-permute-start | bytes 786440 | tf_op jit(solution)/shard_map/ppermute | solution.py:41
  6.1 7.8 %collective-permute-start.3 = (f32[16,4096]{1,0:T(8,128)S(1)}, f32[16,4096]{1,0:T(8,128)S(1)}, u32[]{:S(2)}, u32[]{:S(2)}) collective-permute-start(f32[16,4096]{1,0:T(8,128)S(1)} %get-tuple-element.12.own_ref), channel_id=1, source_target_pairs={{0,1},{1,0},{2,3},{3,2},{4,5},{5,4},{6,7},{7,6},{8,10},{9,11},{10,... | collective-permute-start | bytes 786440 | tf_op jit(solution)/shard_map/ppermute | solution.py:41
  10.8 10.6 %collective-permute-start.8 = (f32[16,4224]{1,0:T(8,128)S(1)}, f32[16,4224]{1,0:T(8,128)S(1)}, u32[]{:S(2)}, u32[]{:S(2)}) collective-permute-start(f32[16,4224]{1,0:T(8,128)S(1)} %shard_map.63.own_ref), channel_id=1, source_target_pairs={{0,4},{1,5},{2,6},{3,7},{4,0},{5,1},{6,2},{7,3},{8,24},{9,25},{10,... | collective-permute-start | bytes 811016 | tf_op jit(solution)/shard_map/ppermute | solution.py:41
  14.3 9.1 %collective-permute-start.4 = (f32[16,4224]{1,0:T(8,128)S(1)}, f32[16,4224]{1,0:T(8,128)S(1)}, u32[]{:S(2)}, u32[]{:S(2)}) collective-permute-start(f32[16,4224]{1,0:T(8,128)S(1)} %shard_map.60.own_ref), channel_id=1, source_target_pairs={{0,2},{1,3},{2,0},{3,1},{4,6},{5,7},{6,4},{7,5},{8,9},{9,8},{10,11... | collective-permute-start | bytes 811016 | tf_op jit(solution)/shard_map/ppermute | solution.py:41
  21.5 6.4 %collective-permute-start.9 = (f32[16,4096]{1,0:T(8,128)S(1)}, f32[16,4096]{1,0:T(8,128)S(1)}, u32[]{:S(2)}, u32[]{:S(2)}) collective-permute-start(f32[16,4096]{1,0:T(8,128)S(1)} %shard_map.64), channel_id=1, source_target_pairs={{0,1},{1,0},{2,3},{3,2},{4,5},{5,4},{6,7},{7,6},{8,10},{9,11},{10,... | collective-permute-start | bytes 786440 | tf_op jit(solution)/shard_map/ppermute | solution.py:41
  23.4 6.4 %collective-permute-start.5 = (f32[16,4096]{1,0:T(8,128)S(1)}, f32[16,4096]{1,0:T(8,128)S(1)}, u32[]{:S(2)}, u32[]{:S(2)}) collective-permute-start(f32[16,4096]{1,0:T(8,128)S(1)} %shard_map.61), channel_id=1, source_target_pairs={{0,16},{1,17},{2,18},{3,19},{4,20},{5,21},{6,22},{7,23},{8,12},{9,... | collective-permute-start | bytes 786440 | tf_op jit(solution)/shard_map/ppermute | solution.py:41
  27.9 9.2 %collective-permute-start.10 = (f32[16,4096]{1,0:T(8,128)S(1)}, f32[16,4096]{1,0:T(8,128)S(1)}, u32[]{:S(2)}, u32[]{:S(2)}) collective-permute-start(f32[16,4096]{1,0:T(8,128)S(1)} %subtract_select_fusion.own_ref.refs_1_), channel_id=1, source_target_pairs={{0,2},{1,3},{2,0},{3,1},{4,6},{5,7},{6,4},{7,5},{8,9},{9,8},{10,11... | collective-permute-start | bytes 786440 | tf_op jit(solution)/shard_map/ppermute | solution.py:41
  29.9 10.1 %collective-permute-start.6 = (f32[16,4096]{1,0:T(8,128)S(1)}, f32[16,4096]{1,0:T(8,128)S(1)}, u32[]{:S(2)}, u32[]{:S(2)}) collective-permute-start(f32[16,4096]{1,0:T(8,128)S(1)} %subtract_select_fusion.1.own_ref.refs_0_), channel_id=1, source_target_pairs={{0,4},{1,5},{2,6},{3,7},{4,0},{5,1},{6,2},{7,3},{8,24},{9,25},{10,... | collective-permute-start | bytes 786440 | tf_op jit(solution)/shard_map/ppermute | solution.py:41
  33.7 11.2 %all-to-all-start = ((f32[32,8,128]{2,1,0:T(8,128)}), f32[32,8,128]{2,1,0:T(8,128)S(1)}, u32[]{:S(2)}, u32[]{:S(2)}) async-start(f32[32,8,128]{2,1,0:T(8,128)} %shard_map.67), calls=%async_computation | async-start | bytes 262144 | tf_op jit(solution)/shard_map/all_to_all | solution.py:339
  37.2 9.2 %collective-permute-start.12 = (f32[8,4096]{1,0:T(8,128)S(1)}, f32[8,4096]{1,0:T(8,128)S(1)}, u32[]{:S(2)}, u32[]{:S(2)}) collective-permute-start(f32[8,4096]{1,0:T(8,128)S(1)} %get-tuple-element.18), channel_id=1, source_target_pairs={{0,8},{1,9},{2,10},{3,11},{4,12},{5,13},{6,14},{7,15},{8,0},{9,1},... | collective-permute-start | bytes 393224 | tf_op jit(solution)/shard_map/ppermute | solution.py:41
  40.1 6.4 %collective-permute-start.11 = (f32[8,4096]{1,0:T(8,128)S(1)}, f32[8,4096]{1,0:T(8,128)S(1)}, u32[]{:S(2)}, u32[]{:S(2)}) collective-permute-start(f32[8,4096]{1,0:T(8,128)S(1)} %get-tuple-element.17), channel_id=1, source_target_pairs={{0,8},{1,9},{2,10},{3,11},{4,12},{5,13},{6,14},{7,15},{8,0},{9,1},... | collective-permute-start | bytes 393224 | tf_op jit(solution)/shard_map/ppermute | solution.py:41

commit v2 on v1

v2 whole, which is shorter than its diff:
```python
import functools
import math

import jax
import jax.numpy as jnp
from jax import lax
from jax.experimental import pallas as pl
from jax.experimental.pallas import tpu as pltpu
from jax.sharding import PartitionSpec as P

AXES = ("grp", "dev")
LANES = 128
ROWS = 8
IN_VMEM = pl.BlockSpec(memory_space=pltpu.VMEM)
IN_SMEM = pl.BlockSpec(memory_space=pltpu.SMEM)
IN_HBM = pl.BlockSpec(memory_space=pltpu.HBM)


def call(body, outputs, in_specs, args, out_specs=None, scratch=()):
    return pl.pallas_call(
        body,
        out_shape=outputs,
        in_specs=in_specs,
        out_specs=jax.tree.map(lambda _: IN_VMEM, outputs) if out_specs is None else out_specs,
        scratch_shapes=scratch,
        compiler_params=pltpu.CompilerParams(vmem_limit_bytes=24 * 1024 * 1024),
    )(*args)


def block(rows, width, dtype=jnp.float32):
    return jax.ShapeDtypeStruct((rows, width), dtype)


def lanes_of(index):
    return slice(index * LANES, (index + 1) * LANES)


def exchange(array, core, masks):
    count = lax.axis_size(AXES)
    route = [(place, place ^ masks[0 if place & core == 0 else 1]) for place in range(count)]
    return lax.ppermute(array, AXES, route)


def chosen_mask(place, core, masks):
    return jnp.where(place & core == 0, masks[0], masks[1])


def three_parts(values):
    high = values.astype(jnp.bfloat16)
    rest = values - high.astype(jnp.float32)
    middle = rest.astype(jnp.bfloat16)
    low = (rest - middle.astype(jnp.float32)).astype(jnp.bfloat16)
    return high, middle, low


def exact_dot(values, table):
    total = None
    for piece in three_parts(values):
        product = jnp.dot(piece, table, preferred_element_type=jnp.float32)
        total = product if total is None else total + product
    return total


def mix(parts):
    left = lax.broadcasted_iota(jnp.int32, (LANES, LANES), 0)
    right = lax.broadcasted_iota(jnp.int32, (LANES, LANES), 1)
    parity = left & right
    for shift in (4, 2, 1):
        parity = parity ^ (parity >> shift)
    table = (1 - 2 * (parity & 1)).astype(jnp.float32).astype(jnp.bfloat16)
    parts = list(parts)
    span = 1
    while span < len(parts):
        for index in range(len(parts)):
            if index & span == 0:
                first, second = parts[index], parts[index | span]
                parts[index], parts[index | span] = first + second, first - second
        span *= 2
    total = exact_dot(jnp.concatenate(parts, axis=0), table)
    rows = parts[0].shape[0]
    return [total[index * rows : (index + 1) * rows] for index in range(len(parts))]


def own_kernel(scaling, core, place_ref, slab_ref, flips_ref, out_ref):
    columns = out_ref.shape[0]
    top = jnp.where(place_ref[0] & core == 0, 0, columns)
    for index in range(flips_ref.shape[0]):
        sign = jnp.where(flips_ref[index : index + 1, :] == 0, scaling, -scaling)
        rows = pl.ds(pl.multiple_of(top, ROWS), columns)
        out_ref[:, lanes_of(index)] = slab_ref[rows, lanes_of(index)] * sign


def split_kernel(scaling, core, place_ref, own_ref, other_ref, flips_ref, offset_ref, *out_refs):
    chunk_refs, spread_ref = out_refs[:-1], out_refs[-1]
    spread_ref[...] = jnp.concatenate([offset_ref[...]] * (LANES // offset_ref.shape[1]), axis=1)
    columns = own_ref.shape[0]
    on_first = place_ref[0] & core == 0
    top = jnp.where(on_first, 0, columns)
    turn = jnp.where(on_first, 1.0, -1.0)
    for index in range(flips_ref.shape[0]):
        here = lanes_of(index)
        sign = jnp.where(flips_ref[index : index + 1, :] == 0, scaling, -scaling)
        for number, chunk_ref in enumerate(chunk_refs):
            own = own_ref[number * ROWS : (number + 1) * ROWS, here]
            other = other_ref[pl.ds(pl.multiple_of(top + number * ROWS, ROWS), ROWS), here] * sign
            chunk_ref[:ROWS, here] = own + other
            chunk_ref[ROWS:, here] = (own - other) * turn


def tile_kernel(core, place_ref, offset_ref, other_offset_ref, tile_ref):
    samples = offset_ref.shape[1]
    own = jnp.concatenate([offset_ref[...]] * (LANES // samples), axis=1)
    lane = lax.broadcasted_iota(jnp.int32, (1, LANES), 1)
    own_first = jnp.where(place_ref[0] & core == 0, 0, 1)
    tile = jnp.where(lane // samples % 2 == own_first, own, other_offset_ref[...])
    tile_ref[...] = jnp.broadcast_to(tile.astype(jnp.float32), tile_ref.shape)


def mix_kernel(core, masks, place_ref, own_ref, other_ref, out_ref):
    slices = own_ref.shape[1] // LANES
    factor = jnp.where(place_ref[0] & chosen_mask(place_ref[0], core, masks) == 0, 1.0, -1.0)
    parts = [
        own_ref[:, lanes_of(index)] * factor + other_ref[:, lanes_of(index)] for index in range(slices)
    ]
    for index, part in enumerate(mix(parts)):
        out_ref[:, lanes_of(index)] = part


def ride_kernel(core, masks, place_ref, own_ref, other_ref, tile_ref, out_ref):
    width = own_ref.shape[1]
    factor = jnp.where(place_ref[0] & chosen_mask(place_ref[0], core, masks) == 0, 1.0, -1.0)
    out_ref[:, :width] = own_ref[...] * factor + other_ref[...]
    for row in range(0, own_ref.shape[0], ROWS):
        out_ref[row : row + ROWS, width:] = tile_ref[...]


def step_kernel(core, masks, place_ref, own_ref, other_ref, out_ref):
    factor = jnp.where(place_ref[0] & chosen_mask(place_ref[0], core, masks) == 0, 1.0, -1.0)
    width = out_ref.shape[1]
    out_ref[...] = own_ref[:, :width] * factor + other_ref[:, :width]


def pick(core, samples, masks, place_ref, tile_ref, chunk_ref, other_ref):
    lane = lax.broadcasted_iota(jnp.int32, (1, LANES), 1)
    place_in = lax.broadcasted_iota(jnp.int32, (LANES, LANES), 0)
    own_chip = lane < 2 * samples
    partner = other_ref[0:1, other_ref.shape[1] - LANES :]
    offsets = jnp.where(own_chip, tile_ref[0:1, :], partner).astype(jnp.int32)
    chosen = jnp.where(place_in == offsets % LANES, 1.0, 0.0).astype(jnp.bfloat16)
    side = jnp.where(place_ref[0] & chosen_mask(place_ref[0], core, masks) == 0, 1.0, -1.0)
    slices = chunk_ref.shape[1] // LANES
    rows = chunk_ref.shape[0]
    stacked = jnp.concatenate([chunk_ref[:, lanes_of(index)] for index in range(slices)], axis=0)
    found = exact_dot(stacked, chosen)
    share = jnp.zeros((rows, LANES), jnp.float32)
    for index in range(slices):
        share = jnp.where(offsets // LANES == index, found[index * rows : (index + 1) * rows], share)
    share = jnp.where(lane // samples % 2 == 0, share[:ROWS], share[ROWS:])
    return share * jnp.where(own_chip, side, 1.0)


def pick_kernel(core, samples, masks, place_ref, tile_ref, chunk_ref, other_ref, out_ref):
    out_ref[...] = pick(core, samples, masks, place_ref, tile_ref, chunk_ref, other_ref)


def pick_all_kernel(core, masks, place_ref, tile_ref, chunk_ref, other_ref, early_ref, out_ref):
    samples = out_ref.shape[1] * 2
    late = pick(core, samples, masks, place_ref, tile_ref, chunk_ref, other_ref)
    turned = jnp.concatenate([late, early_ref[...]], axis=0).T
    half = samples // 2
    starts = [
        (chip * 2 + second) * samples + part * half for part in range(2) for second in range(2) for chip in range(2)
    ]
    tile = jnp.concatenate([turned[start : start + half] for start in starts], axis=1)
    for place in range(out_ref.shape[0]):
        out_ref[place] = tile


def gram_kernel(core, all_masks, place_ref, shares_ref, after_ref, gram_ref, sketch_ref):
    count, rows, _ = shares_ref.shape
    columns = gram_ref.shape[0]
    width = columns // 2
    lane = lax.broadcasted_iota(jnp.int32, (rows, LANES), 1)
    number = lane % width // ROWS

    def of_core(place, second):
        others = shares_ref[place ^ all_masks[0][second]]
        for chunk in range(1, len(all_masks)):
            others = jnp.where(number == chunk, shares_ref[place ^ all_masks[chunk][second]], others)
        return shares_ref[place] + pltpu.roll(others, LANES - width, 1)

    def of_chip(place):
        second = pltpu.roll(of_core(place | core, 1), width, 1)
        return jnp.where(lane % columns < width, of_core(place, 0), second)

    chips = [place for place in range(count) if place & core == 0]
    stacked = jnp.concatenate([of_chip(place) for place in chips], axis=0)
    parts = [slice(start, start + columns) for start in range(0, LANES, columns)]
    products = lax.dot_general(
        stacked,
        stacked,
        (((0,), (0,)), ((), ())),
        precision=lax.Precision.HIGHEST,
        preferred_element_type=jnp.float32,
    )
    gram = sum([products[part, part] for part in parts[1:]], products[parts[0], parts[0]])
    gram_ref[...] = gram * (1.0 / (count * 2 * rows))
    own = of_chip(place_ref[0] & ~core)
    on_first = place_ref[0] & core == 0
    for half in range(2):
        first, second = own[:, parts[half * 2]], own[:, parts[half * 2 + 1]]
        sketch_ref[half * rows : (half + 1) * rows] = jnp.where(on_first, first, second)


def last_kernel(core, masks, place_ref, own_ref, other_ref, keep_ref, send_ref):
    on_first = place_ref[0] & core == 0
    factor = jnp.where(place_ref[0] & chosen_mask(place_ref[0], core, masks) == 0, 1.0, -1.0)
    for out_ref, top in ((keep_ref, jnp.where(on_first, 0, ROWS)), (send_ref, jnp.where(on_first, ROWS, 0))):
        rows = pl.ds(pl.multiple_of(top, ROWS), ROWS)
        out_ref[...] = own_ref[rows, :] * factor + other_ref[rows, :]


def join_kernel(core, place_ref, *refs):
    block_refs, (whole_ref, token_ref, sems) = refs[:-3], refs[-3:]
    token_ref[...] = jnp.zeros_like(token_ref)
    on_first = place_ref[0] & core == 0
    half = whole_ref.shape[0] // 2
    tops = []
    for kept in (True, False):
        base = jnp.where(on_first, 0, half) if kept else jnp.where(on_first, half, 0)
        tops += [base + row for row in range(0, half, ROWS)]
    copies = [
        pltpu.make_async_copy(
            block_ref, whole_ref.at[pl.ds(pl.multiple_of(top, ROWS), ROWS)], sems.at[number]
        )
        for number, (block_ref, top) in enumerate(zip(block_refs, tops))
    ]
    for copy in copies:
        copy.start()
    for copy in copies:
        copy.wait()


def local_any(matrix_slab, sign_flips, sample_offset):
    columns, local_rows = matrix_slab.shape
    count = lax.axis_size(AXES)
    samples = sample_offset.shape[0]
    numbers = jnp.arange(local_rows, dtype=jnp.int32)

    def table(order):
        common = numbers[:order, None] & numbers[None, :order]
        return (1 - 2 * (lax.population_count(common) & 1)).astype(jnp.float32)

    signs = (1 - 2 * sign_flips).astype(jnp.float32) * jnp.float32(1.0 / math.sqrt(local_rows * count))
    outer = local_rows // LANES
    shaped = (matrix_slab * signs[None, :]).reshape(columns, outer, LANES)
    shaped = jnp.einsum("cak,kz->caz", shaped, table(LANES), precision=lax.Precision.HIGHEST)
    shaped = jnp.einsum("cak,az->czk", shaped, table(outer), precision=lax.Precision.HIGHEST)
    current = shaped.reshape(columns, local_rows)
    for bit in range(count.bit_length() - 1):
        other = exchange(current, 1, (1 << bit, 1 << bit))
        lower = lax.axis_index(AXES) & 1 << bit == 0
        current = jnp.where(lower, current + other, other - current)
    sketch = jnp.take(current, sample_offset, axis=1)
    gram = jnp.dot(sketch, sketch.T, precision=lax.Precision.HIGHEST)
    return (current, sketch, lax.psum(gram, AXES) / jnp.float32(samples * count))


def local(matrix_slab, sign_flips, sample_offset):
    columns, local_rows = matrix_slab.shape
    grp_bits = lax.axis_size("grp").bit_length() - 1
    dev_bits = lax.axis_size("dev").bit_length() - 1
    count = lax.axis_size(AXES)
    samples = sample_offset.shape[0]
    if (grp_bits, dev_bits, columns, samples) != (2, 3, 4 * ROWS, 2 * ROWS):
        return local_any(matrix_slab, sign_flips, sample_offset)
    place = lax.axis_index(AXES).astype(jnp.int32).reshape(1)
    flips = sign_flips.reshape(local_rows // LANES, LANES)
    offsets = sample_offset.reshape(1, samples)
    y, z_low, z_high, core, x = (1 << bit for bit in range(dev_bits + grp_bits))
    scaling = 1.0 / math.sqrt(local_rows * count)
    across = (core, core)
    orders = [
        [(y, z_low), (x, z_high), (z_high, y), (z_low, x)],
        [(x, z_high), (y, z_low), (z_low, x), (z_high, y)],
    ]

    other = exchange(matrix_slab, core, across)
    other_flips = exchange(flips, core, across)
    other_offsets = exchange(offsets, core, across)
    own = call(
        functools.partial(own_kernel, scaling, core),
        block(columns // 2, local_rows),
        [IN_SMEM, IN_VMEM, IN_VMEM],
        [place, matrix_slab, flips],
    )
    chunk = block(2 * ROWS, local_rows)
    *chunks, spread = call(
        functools.partial(split_kernel, scaling, core),
        [chunk, chunk, block(1, LANES, jnp.int32)],
        [IN_SMEM] + [IN_VMEM] * 4,
        [place, own, other, other_flips, other_offsets],
    )
    tile = call(
        functools.partial(tile_kernel, core),
        block(ROWS, LANES),
        [IN_SMEM] + [IN_VMEM] * 2,
        [place, offsets, spread],
    )
    ridden, thirds = [], []
    for current, order in zip(chunks, orders):
        current = call(
            functools.partial(mix_kernel, core, order[0]),
            chunk,
            [IN_SMEM] + [IN_VMEM] * 2,
            [place, current, exchange(current, core, order[0])],
        )
        current = call(
            functools.partial(ride_kernel, core, order[1]),
            block(2 * ROWS, local_rows + LANES),
            [IN_SMEM] + [IN_VMEM] * 3,
            [place, current, exchange(current, core, order[1]), tile],
        )
        partner = exchange(current, core, order[2])
        ridden.append(partner)
        thirds.append(
            call(
                functools.partial(step_kernel, core, order[2]),
                chunk,
                [IN_SMEM] + [IN_VMEM] * 2,
                [place, current, partner],
            )
        )
    first, second = thirds
    last_masks = [order[3] for order in orders]
    early = call(
        functools.partial(pick_kernel, core, samples, last_masks[1]),
        block(ROWS, LANES),
        [IN_SMEM] + [IN_VMEM] * 3,
        [place, tile, second, ridden[0]],
    )
    shares = call(
        functools.partial(pick_all_kernel, core, last_masks[0]),
        jax.ShapeDtypeStruct((count, samples // 2, LANES), jnp.float32),
        [IN_SMEM] + [IN_VMEM] * 4,
        [place, tile, first, ridden[1], early],
    )
    lasts = [
        call(
            functools.partial(last_kernel, core, masks),
            [block(ROWS, local_rows)] * 2,
            [IN_SMEM] + [IN_VMEM] * 2,
            [place, current, exchange(current, core, masks)],
        )
        for current, masks in zip((first, second), last_masks)
    ]
    kept = [keep for keep, _ in lasts]
    back = [exchange(send, core, across) for _, send in lasts]
    transformed, token = call(
        functools.partial(join_kernel, core),
        [block(columns, local_rows), block(ROWS, LANES)],
        [IN_SMEM] + [IN_VMEM] * 4,
        [place, *kept, *back],
        out_specs=[IN_HBM, IN_VMEM],
        scratch=[pltpu.SemaphoreType.DMA((4,))],
    )
    gram, sketch = call(
        functools.partial(gram_kernel, core, last_masks),
        [block(columns, columns), block(samples, columns)],
        [IN_SMEM, IN_VMEM, IN_VMEM],
        [place, lax.all_to_all(shares, AXES, 0, 0, tiled=True), token],
    )
    return (transformed, sketch.T, gram)


def solution(mesh):
    return jax.shard_map(
        local,
        mesh=mesh,
        in_specs=(P(None, AXES), P(AXES), P(AXES)),
        out_specs=(P(None, AXES), P(None, AXES), P()),
        check_vma=False,
    )
```

time: 47.5 us -> 46.1 us (0.971)
  starting transfers between devices: 21 us -> 20.1 us
    ppermute x13, starting transfers between devices: 17.5 us -> 15.1 us  [exchange(): return lax.ppermute(array, AXES, route)]
    ppermute x13, waiting for transfers between devices: 14.9 us -> 16.8 us  [exchange(): return lax.ppermute(array, AXES, route)]
    all_to_all x1, waiting for transfers between devices: 4.75 us -> 2.95 us  [local(): lax.all_to_all(shares, AXES, 0, 0, tiled=True)]
    all_to_all x1, starting transfers between devices: 3.49 us -> 4.97 us  [local(): lax.all_to_all(shares, AXES, 0, 0, tiled=True)]
    pallas_call x11 -> x15, Pallas kernels: 4.42 us -> 4.26 us  [call(): pl.pallas_call(body, out_shape=outputs, in_specs=in_specs, out_specs=jax....]
  transfers between devices with their start and end apart: 14 -> 14, of which waited for: 7 -> 10; matrix products, arithmetic and copies ran while one was open for 0% -> 0% of each run, Pallas kernels for 7% -> 7%
where the time goes in v2:
time: 46.1 us; the launch traced here: 45.9 us
  starting transfers between devices  20.1 us (44%)
  waiting for transfers between devices  19.7 us (43%)
  Pallas kernels  4.26 us (9%)
  local copies, waits for them, and re-layouts  1.05 us (2%)
  between operations  0.74 us (2%)
    ppermute x13, waiting for transfers between devices, exchange(): return lax.ppermute(array, AXES, route)  16.8 us
    ppermute x13, starting transfers between devices, exchange(): return lax.ppermute(array, AXES, route)  15.1 us
    all_to_all x1, starting transfers between devices, local(): lax.all_to_all(shares, AXES, 0, 0, tiled=True)  4.97 us
    pallas_call x15, Pallas kernels, call(): pl.pallas_call(body, out_shape=outputs, in_specs=in_specs, out_specs=jax....  4.26 us
    all_to_all x1, waiting for transfers between devices, local(): lax.all_to_all(shares, AXES, 0, 0, tiled=True)  2.95 us
    unnamed x6, local copies, waits for them, and re-layouts  1.05 us
  transfers between devices with their start and end apart: 14, of which 10 were waited for; matrix products, arithmetic and copies ran while one was open for 0% of the time, Pallas kernels for 7%

profile of v2, /device:TPU:0, one launch (start us, length us, event | category | flops | bytes accessed | tf_op | source)
XLA Modules:
  0.0 45.9 jit_solution(820050092166827719)
XLA Ops:
  0.6 0.5 %collective-permute-start = (f32[32,4096]{1,0:T(8,128)}, f32[32,4096]{1,0:T(8,128)S(1)}, u32[]{:S(2)}, u32[]{:S(2)}) collective-permute-start(f32[32,4096]{1,0:T(8,128)} %slab_ref.1), channel_id=1, source_target_pairs={{0,8},{1,9},{2,10},{3,11},{4,12},{5,13},{6,14},{7,15},{8,0},{9,1},... | collective-permute-start | bytes 1572872 | tf_op jit(solution)/shard_map/ppermute | solution.py:41
  1.2 0.4 collective-permute-start.2
  1.7 1.0 %copy-done = f32[32,4096]{1,0:T(8,128)S(1)} copy-done((f32[32,4096]{1,0:T(8,128)S(1)}, f32[32,4096]{1,0:T(8,128)}, u32[]{:S(2)}) %copy-start) | copy-done | bytes 524312
  3.0 2.9 %collective-permute-start.7 = (f32[16,4096]{1,0:T(8,128)S(1)}, f32[16,4096]{1,0:T(8,128)S(1)}, u32[]{:S(2)}, u32[]{:S(2)}) collective-permute-start(f32[16,4096]{1,0:T(8,128)S(1)} %get-tuple-element.17.own_ref), channel_id=1, source_target_pairs={{0,16},{1,17},{2,18},{3,19},{4,20},{5,21},{6,22},{7,23},{8,12},{9,... | collective-permute-start | bytes 786440 | tf_op jit(solution)/shard_map/ppermute | solution.py:41
  5.9 1.5 %collective-permute-start.3 = (f32[16,4096]{1,0:T(8,128)S(1)}, f32[16,4096]{1,0:T(8,128)S(1)}, u32[]{:S(2)}, u32[]{:S(2)}) collective-permute-start(f32[16,4096]{1,0:T(8,128)S(1)} %get-tuple-element.14.own_ref), channel_id=1, source_target_pairs={{0,1},{1,0},{2,3},{3,2},{4,5},{5,4},{6,7},{7,6},{8,10},{9,11},{10,... | collective-permute-start | bytes 786440 | tf_op jit(solution)/shard_map/ppermute | solution.py:41
  7.4 2.8 %collective-permute-done.7.other_ref = f32[16,4096]{1,0:T(8,128)S(1)} collective-permute-done((f32[16,4096]{1,0:T(8,128)S(1)}, f32[16,4096]{1,0:T(8,128)S(1)}, u32[]{:S(2)}, u32[]{:S(2)}) %collective-permute-start.7) | collective-permute-done | bytes 262176 | tf_op jit(solution)/shard_map/ppermute | solution.py:41
  10.3 0.3 shard_map.65.own_ref
  10.6 2.1 %collective-permute-start.8 = (f32[16,4096]{1,0:T(8,128)S(1)}, f32[16,4096]{1,0:T(8,128)S(1)}, u32[]{:S(2)}, u32[]{:S(2)}) collective-permute-start(f32[16,4096]{1,0:T(8,128)S(1)} %shard_map.65.own_ref), channel_id=1, source_target_pairs={{0,1},{1,0},{2,3},{3,2},{4,5},{5,4},{6,7},{7,6},{8,10},{9,11},{10,... | collective-permute-start | bytes 786440 | tf_op jit(solution)/shard_map/ppermute | solution.py:41
  12.7 0.3 shard_map.60.own_ref
  13.0 1.6 %collective-permute-start.4 = (f32[16,4096]{1,0:T(8,128)S(1)}, f32[16,4096]{1,0:T(8,128)S(1)}, u32[]{:S(2)}, u32[]{:S(2)}) collective-permute-start(f32[16,4096]{1,0:T(8,128)S(1)} %shard_map.60.own_ref), channel_id=1, source_target_pairs={{0,16},{1,17},{2,18},{3,19},{4,20},{5,21},{6,22},{7,23},{8,12},{9,... | collective-permute-start | bytes 786440 | tf_op jit(solution)/shard_map/ppermute | solution.py:41
  14.7 2.4 %collective-permute-done.8.other_ref = f32[16,4096]{1,0:T(8,128)S(1)} collective-permute-done((f32[16,4096]{1,0:T(8,128)S(1)}, f32[16,4096]{1,0:T(8,128)S(1)}, u32[]{:S(2)}, u32[]{:S(2)}) %collective-permute-start.8) | collective-permute-done | bytes 262176 | tf_op jit(solution)/shard_map/ppermute | solution.py:41
  17.1 2.1 %collective-permute-start.9 = (f32[16,4224]{1,0:T(8,128)S(1)}, f32[16,4224]{1,0:T(8,128)S(1)}, u32[]{:S(2)}, u32[]{:S(2)}) collective-permute-start(f32[16,4224]{1,0:T(8,128)S(1)} %shard_map.66.own_ref), channel_id=1, source_target_pairs={{0,2},{1,3},{2,0},{3,1},{4,6},{5,7},{6,4},{7,5},{8,24},{9,25},{10,... | collective-permute-start | bytes 811016 | tf_op jit(solution)/shard_map/ppermute | solution.py:41
  19.5 2.7 %collective-permute-start.5 = (f32[16,4224]{1,0:T(8,128)S(1)}, f32[16,4224]{1,0:T(8,128)S(1)}, u32[]{:S(2)}, u32[]{:S(2)}) collective-permute-start(f32[16,4224]{1,0:T(8,128)S(1)} %shard_map.62.own_ref), channel_id=1, source_target_pairs={{0,4},{1,5},{2,6},{3,7},{4,0},{5,1},{6,2},{7,3},{8,9},{9,8},{10,11... | collective-permute-start | bytes 811016 | tf_op jit(solution)/shard_map/ppermute | solution.py:41
  22.2 5.2 %collective-permute-done.9.other_ref = f32[16,4224]{1,0:T(8,128)S(1)} collective-permute-done((f32[16,4224]{1,0:T(8,128)S(1)}, f32[16,4224]{1,0:T(8,128)S(1)}, u32[]{:S(2)}, u32[]{:S(2)}) %collective-permute-start.9) | collective-permute-done | bytes 270368 | tf_op jit(solution)/shard_map/ppermute | solution.py:41
  27.4 0.8 %collective-permute-start.10 = (f32[16,4096]{1,0:T(8,128)S(1)}, f32[16,4096]{1,0:T(8,128)S(1)}, u32[]{:S(2)}, u32[]{:S(2)}) collective-permute-start(f32[16,4096]{1,0:T(8,128)S(1)} %shard_map.67.own_ref.chunk_ref), channel_id=1, source_target_pairs={{0,4},{1,5},{2,6},{3,7},{4,0},{5,1},{6,2},{7,3},{8,9},{9,8},{10,11... | collective-permute-start | bytes 786440 | tf_op jit(solution)/shard_map/ppermute | solution.py:41
  28.1 2.3 %collective-permute-done.5.other_ref = f32[16,4224]{1,0:T(8,128)S(1)} collective-permute-done((f32[16,4224]{1,0:T(8,128)S(1)}, f32[16,4224]{1,0:T(8,128)S(1)}, u32[]{:S(2)}, u32[]{:S(2)}) %collective-permute-start.5) | collective-permute-done | bytes 270368 | tf_op jit(solution)/shard_map/ppermute | solution.py:41
  30.4 0.3 collective-permute-start.6
  31.0 1.1 %shard_map.71 = f32[32,8,128]{2,1,0:T(8,128)} custom-call(s32[1]{0:T(128)} %bitcast.place_ref, f32[8,128]{1,0:T(8,128)S(1)} %shard_map.61.tile_ref, f32[16,4096]{1,0:T(8,128)S(1)} %shard_map.63.own_ref.chunk_ref, f32[16,4224]{1,0:T(8,128)S(1)} %collective-permute-done.9.other_ref, f32[8,128]{1,0:T(8,128)S(1)} %shard_map.70.early_ref), custom_call_target="tpu_custom_call" | custom-call | tf_op jit(solution)/shard_map/pallas_call | solution.py:20
  32.1 5.0 %all-to-all-start = ((f32[32,8,128]{2,1,0:T(8,128)}), f32[32,8,128]{2,1,0:T(8,128)S(1)}, u32[]{:S(2)}, u32[]{:S(2)}) async-start(f32[32,8,128]{2,1,0:T(8,128)} %shard_map.71), calls=%async_computation | async-start | bytes 262144 | tf_op jit(solution)/shard_map/all_to_all | solution.py:371
  37.4 2.1 %collective-permute-done.6.other_ref = f32[16,4096]{1,0:T(8,128)S(1)} collective-permute-done((f32[16,4096]{1,0:T(8,128)S(1)}, f32[16,4096]{1,0:T(8,128)S(1)}, u32[]{:S(2)}, u32[]{:S(2)}) %collective-permute-start.6) | collective-permute-done | bytes 262176 | tf_op jit(solution)/shard_map/ppermute | solution.py:41
  39.7 1.3 %collective-permute-done.11.refs_2_ = f32[8,4096]{1,0:T(8,128)S(1)} collective-permute-done((f32[8,4096]{1,0:T(8,128)S(1)}, f32[8,4096]{1,0:T(8,128)S(1)}, u32[]{:S(2)}, u32[]{:S(2)}) %collective-permute-start.11) | collective-permute-done | bytes 131104 | tf_op jit(solution)/shard_map/ppermute | solution.py:41
  41.0 0.8 %shard_map.69 = (f32[32,4096]{1,0:T(8,128)}, f32[8,128]{1,0:T(8,128)S(1)}) custom-call(s32[1]{0:T(128)} %bitcast.place_ref, f32[8,4096]{1,0:T(8,128)S(1)} %get-tuple-element.16.refs_0_, f32[8,4096]{1,0:T(8,128)S(1)} %get-tuple-element.18.refs_1_, f32[8,4096]{1,0:T(8,128)S(1)} %collective-permute-done.11.refs_2_, f32[8,4096]{1,0:T(8,128)S(1)} %collective-permute-done.12.refs_3_), custom_call_target="tpu_custom_call" | custom-call | tf_op jit(solution)/shard_map/pallas_call | solution.py:20
  41.9 2.9 %all-to-all-done.shares_ref = f32[32,8,128]{2,1,0:T(8,128)S(1)} async-done(((f32[32,8,128]{2,1,0:T(8,128)}), f32[32,8,128]{2,1,0:T(8,128)S(1)}, u32[]{:S(2)}, u32[]{:S(2)}) %all-to-all-start) | async-done | bytes 131104 | tf_op jit(solution)/shard_map/all_to_all | solution.py:371
  44.8 1.1 %shard_map.72 = (f32[32,32]{1,0:T(8,128)}, f32[16,32]{1,0:T(8,128)}) custom-call(s32[1]{0:T(128)} %bitcast.place_ref, f32[32,8,128]{2,1,0:T(8,128)S(1)} %all-to-all-done.shares_ref, f32[8,128]{1,0:T(8,128)S(1)} %get-tuple-element.22.after_ref), custom_call_target="tpu_custom_call" | custom-call | tf_op jit(solution)/shard_map/pallas_call | solution.py:20
  (25 shorter events, 1.6 us)
Async XLA Ops:
  0.6 1.0 %copy-start.1 = (s32[4096]{0:T(1024)S(1)}, s32[4096]{0:T(1024)}, u32[]{:S(2)}) copy-start(s32[4096]{0:T(1024)} %param.4) | copy-start | bytes 49156
  0.6 2.3 %collective-permute-start = (f32[32,4096]{1,0:T(8,128)}, f32[32,4096]{1,0:T(8,128)S(1)}, u32[]{:S(2)}, u32[]{:S(2)}) collective-permute-start(f32[32,4096]{1,0:T(8,128)} %slab_ref.1), channel_id=1, source_target_pairs={{0,8},{1,9},{2,10},{3,11},{4,12},{5,13},{6,14},{7,15},{8,0},{9,1},... | collective-permute-start | bytes 1572872 | tf_op jit(solution)/shard_map/ppermute | solution.py:41
  1.2 1.8 %collective-permute-start.1 = (s32[32,128]{1,0:T(8,128)}, s32[32,128]{1,0:T(8,128)S(1)}, u32[]{:S(2)}, u32[]{:S(2)}) collective-permute-start(s32[32,128]{1,0:T(8,128)} %bitcast.4), channel_id=1, source_target_pairs={{0,8},{1,9},{2,10},{3,11},{4,12},{5,13},{6,14},{7,15},{8,0},{9,1},... | collective-permute-start | bytes 49160 | tf_op jit(solution)/shard_map/ppermute | solution.py:41
  1.2 1.7 %collective-permute-start.2 = (s32[1,16]{1,0:T(1,128)}, s32[1,16]{1,0:T(1,128)S(1)}, u32[]{:S(2)}, u32[]{:S(2)}) collective-permute-start(s32[1,16]{1,0:T(1,128)} %bitcast.6), channel_id=1, source_target_pairs={{0,8},{1,9},{2,10},{3,11},{4,12},{5,13},{6,14},{7,15},{8,0},{9,1},... | collective-permute-start | bytes 200 | tf_op jit(solution)/shard_map/ppermute | solution.py:41
  1.7 1.0 %copy-start = (f32[32,4096]{1,0:T(8,128)S(1)}, f32[32,4096]{1,0:T(8,128)}, u32[]{:S(2)}) copy-start(f32[32,4096]{1,0:T(8,128)} %slab_ref.1) | copy-start | bytes 1572868
  3.0 7.3 %collective-permute-start.7 = (f32[16,4096]{1,0:T(8,128)S(1)}, f32[16,4096]{1,0:T(8,128)S(1)}, u32[]{:S(2)}, u32[]{:S(2)}) collective-permute-start(f32[16,4096]{1,0:T(8,128)S(1)} %get-tuple-element.17.own_ref), channel_id=1, source_target_pairs={{0,16},{1,17},{2,18},{3,19},{4,20},{5,21},{6,22},{7,23},{8,12},{9,... | collective-permute-start | bytes 786440 | tf_op jit(solution)/shard_map/ppermute | solution.py:41
  5.9 6.8 %collective-permute-start.3 = (f32[16,4096]{1,0:T(8,128)S(1)}, f32[16,4096]{1,0:T(8,128)S(1)}, u32[]{:S(2)}, u32[]{:S(2)}) collective-permute-start(f32[16,4096]{1,0:T(8,128)S(1)} %get-tuple-element.14.own_ref), channel_id=1, source_target_pairs={{0,1},{1,0},{2,3},{3,2},{4,5},{5,4},{6,7},{7,6},{8,10},{9,11},{10,... | collective-permute-start | bytes 786440 | tf_op jit(solution)/shard_map/ppermute | solution.py:41
  10.6 6.5 %collective-permute-start.8 = (f32[16,4096]{1,0:T(8,128)S(1)}, f32[16,4096]{1,0:T(8,128)S(1)}, u32[]{:S(2)}, u32[]{:S(2)}) collective-permute-start(f32[16,4096]{1,0:T(8,128)S(1)} %shard_map.65.own_ref), channel_id=1, source_target_pairs={{0,1},{1,0},{2,3},{3,2},{4,5},{5,4},{6,7},{7,6},{8,10},{9,11},{10,... | collective-permute-start | bytes 786440 | tf_op jit(solution)/shard_map/ppermute | solution.py:41
  13.0 1.6 %copy-start.2 = (s32[16]{0:T(128)S(1)}, s32[16]{0:T(128)}, u32[]{:S(2)}) copy-start(s32[16]{0:T(128)} %param.5) | copy-start | bytes 196
  13.0 6.4 %collective-permute-start.4 = (f32[16,4096]{1,0:T(8,128)S(1)}, f32[16,4096]{1,0:T(8,128)S(1)}, u32[]{:S(2)}, u32[]{:S(2)}) collective-permute-start(f32[16,4096]{1,0:T(8,128)S(1)} %shard_map.60.own_ref), channel_id=1, source_target_pairs={{0,16},{1,17},{2,18},{3,19},{4,20},{5,21},{6,22},{7,23},{8,12},{9,... | collective-permute-start | bytes 786440 | tf_op jit(solution)/shard_map/ppermute | solution.py:41
  17.1 10.2 %collective-permute-start.9 = (f32[16,4224]{1,0:T(8,128)S(1)}, f32[16,4224]{1,0:T(8,128)S(1)}, u32[]{:S(2)}, u32[]{:S(2)}) collective-permute-start(f32[16,4224]{1,0:T(8,128)S(1)} %shard_map.66.own_ref), channel_id=1, source_target_pairs={{0,2},{1,3},{2,0},{3,1},{4,6},{5,7},{6,4},{7,5},{8,24},{9,25},{10,... | collective-permute-start | bytes 811016 | tf_op jit(solution)/shard_map/ppermute | solution.py:41
  19.5 10.9 %collective-permute-start.5 = (f32[16,4224]{1,0:T(8,128)S(1)}, f32[16,4224]{1,0:T(8,128)S(1)}, u32[]{:S(2)}, u32[]{:S(2)}) collective-permute-start(f32[16,4224]{1,0:T(8,128)S(1)} %shard_map.62.own_ref), channel_id=1, source_target_pairs={{0,4},{1,5},{2,6},{3,7},{4,0},{5,1},{6,2},{7,3},{8,9},{9,8},{10,11... | collective-permute-start | bytes 811016 | tf_op jit(solution)/shard_map/ppermute | solution.py:41
  27.4 10.0 %collective-permute-start.10 = (f32[16,4096]{1,0:T(8,128)S(1)}, f32[16,4096]{1,0:T(8,128)S(1)}, u32[]{:S(2)}, u32[]{:S(2)}) collective-permute-start(f32[16,4096]{1,0:T(8,128)S(1)} %shard_map.67.own_ref.chunk_ref), channel_id=1, source_target_pairs={{0,4},{1,5},{2,6},{3,7},{4,0},{5,1},{6,2},{7,3},{8,9},{9,8},{10,11... | collective-permute-start | bytes 786440 | tf_op jit(solution)/shard_map/ppermute | solution.py:41
  30.4 9.1 %collective-permute-start.6 = (f32[16,4096]{1,0:T(8,128)S(1)}, f32[16,4096]{1,0:T(8,128)S(1)}, u32[]{:S(2)}, u32[]{:S(2)}) collective-permute-start(f32[16,4096]{1,0:T(8,128)S(1)} %shard_map.63.own_ref.chunk_ref), channel_id=1, source_target_pairs={{0,2},{1,3},{2,0},{3,1},{4,6},{5,7},{6,4},{7,5},{8,24},{9,25},{10,... | collective-permute-start | bytes 786440 | tf_op jit(solution)/shard_map/ppermute | solution.py:41
  32.1 12.7 %all-to-all-start = ((f32[32,8,128]{2,1,0:T(8,128)}), f32[32,8,128]{2,1,0:T(8,128)S(1)}, u32[]{:S(2)}, u32[]{:S(2)}) async-start(f32[32,8,128]{2,1,0:T(8,128)} %shard_map.71), calls=%async_computation | async-start | bytes 262144 | tf_op jit(solution)/shard_map/all_to_all | solution.py:371
  37.4 2.3 %collective-permute-start.12 = (f32[8,4096]{1,0:T(8,128)S(1)}, f32[8,4096]{1,0:T(8,128)S(1)}, u32[]{:S(2)}, u32[]{:S(2)}) collective-permute-start(f32[8,4096]{1,0:T(8,128)S(1)} %get-tuple-element.20), channel_id=1, source_target_pairs={{0,8},{1,9},{2,10},{3,11},{4,12},{5,13},{6,14},{7,15},{8,0},{9,1},... | collective-permute-start | bytes 393224 | tf_op jit(solution)/shard_map/ppermute | solution.py:41
  39.6 1.4 %collective-permute-start.11 = (f32[8,4096]{1,0:T(8,128)S(1)}, f32[8,4096]{1,0:T(8,128)S(1)}, u32[]{:S(2)}, u32[]{:S(2)}) collective-permute-start(f32[8,4096]{1,0:T(8,128)S(1)} %get-tuple-element.19), channel_id=1, source_target_pairs={{0,8},{1,9},{2,10},{3,11},{4,12},{5,13},{6,14},{7,15},{8,0},{9,1},... | collective-permute-start | bytes 393224 | tf_op jit(solution)/shard_map/ppermute | solution.py:41

commit v3 on v2

--- a/solution.py
+++ b/solution.py
@@ -43,6 +43,12 @@
 
 def chosen_mask(place, core, masks):
     return jnp.where(place & core == 0, masks[0], masks[1])
+
+
+def combine(current, partner, core, masks):
+    place = lax.axis_index(AXES)
+    lower = place & chosen_mask(place, core, masks) == 0
+    return jnp.where(lower, current + partner, partner - current)
 
 
 def three_parts(values):
@@ -116,7 +122,7 @@
     tile_ref[...] = jnp.broadcast_to(tile.astype(jnp.float32), tile_ref.shape)
 
 
-def mix_kernel(core, masks, place_ref, own_ref, other_ref, out_ref):
+def mix_kernel(core, masks, place_ref, own_ref, other_ref, tile_ref, out_ref):
     slices = own_ref.shape[1] // LANES
     factor = jnp.where(place_ref[0] & chosen_mask(place_ref[0], core, masks) == 0, 1.0, -1.0)
     parts = [
@@ -124,20 +130,18 @@
     ]
     for index, part in enumerate(mix(parts)):
         out_ref[:, lanes_of(index)] = part
-
-
-def ride_kernel(core, masks, place_ref, own_ref, other_ref, tile_ref, out_ref):
-    width = own_ref.shape[1]
-    factor = jnp.where(place_ref[0] & chosen_mask(place_ref[0], core, masks) == 0, 1.0, -1.0)
-    out_ref[:, :width] = own_ref[...] * factor + other_ref[...]
     for row in range(0, own_ref.shape[0], ROWS):
-        out_ref[row : row + ROWS, width:] = tile_ref[...]
+        out_ref[row : row + ROWS, lanes_of(slices)] = tile_ref[...]
 
 
 def step_kernel(core, masks, place_ref, own_ref, other_ref, out_ref):
     factor = jnp.where(place_ref[0] & chosen_mask(place_ref[0], core, masks) == 0, 1.0, -1.0)
     width = out_ref.shape[1]
     out_ref[...] = own_ref[:, :width] * factor + other_ref[:, :width]
+
+
+def step_after_kernel(core, masks, place_ref, own_ref, other_ref, after_ref, out_ref):
+    step_kernel(core, masks, place_ref, own_ref, other_ref, out_ref)
 
 
 def pick(core, samples, masks, place_ref, tile_ref, chunk_ref, other_ref):
@@ -163,53 +167,57 @@
     out_ref[...] = pick(core, samples, masks, place_ref, tile_ref, chunk_ref, other_ref)
 
 
-def pick_all_kernel(core, masks, place_ref, tile_ref, chunk_ref, other_ref, early_ref, out_ref):
-    samples = out_ref.shape[1] * 2
+def pick_all_kernel(core, samples, masks, place_ref, tile_ref, chunk_ref, other_ref, early_ref, out_ref):
     late = pick(core, samples, masks, place_ref, tile_ref, chunk_ref, other_ref)
-    turned = jnp.concatenate([late, early_ref[...]], axis=0).T
-    half = samples // 2
-    starts = [
-        (chip * 2 + second) * samples + part * half for part in range(2) for second in range(2) for chip in range(2)
-    ]
-    tile = jnp.concatenate([turned[start : start + half] for start in starts], axis=1)
+    lane = lax.broadcasted_iota(jnp.int32, late.shape, 1)
+    tile = jnp.where(lane < LANES // 2, late, pltpu.roll(early_ref[...], LANES // 2, 1))
     for place in range(out_ref.shape[0]):
         out_ref[place] = tile
 
 
 def gram_kernel(core, all_masks, place_ref, shares_ref, after_ref, gram_ref, sketch_ref):
     count, rows, _ = shares_ref.shape
-    columns = gram_ref.shape[0]
-    width = columns // 2
+    samples = sketch_ref.shape[0]
+    width, half = 2 * samples, LANES // 2
     lane = lax.broadcasted_iota(jnp.int32, (rows, LANES), 1)
-    number = lane % width // ROWS
 
     def of_core(place, second):
-        others = shares_ref[place ^ all_masks[0][second]]
-        for chunk in range(1, len(all_masks)):
-            others = jnp.where(number == chunk, shares_ref[place ^ all_masks[chunk][second]], others)
-        return shares_ref[place] + pltpu.roll(others, LANES - width, 1)
-
-    def of_chip(place):
-        second = pltpu.roll(of_core(place | core, 1), width, 1)
-        return jnp.where(lane % columns < width, of_core(place, 0), second)
+        first, last = (shares_ref[place ^ masks[second]] for masks in all_masks)
+        return shares_ref[place] + pltpu.roll(jnp.where(lane < half, first, last), LANES - width, 1)
+
+    def moved(values, start):
+        return pltpu.roll(values, start, 1) if start % LANES else values
 
     chips = [place for place in range(count) if place & core == 0]
-    stacked = jnp.concatenate([of_chip(place) for place in chips], axis=0)
-    parts = [slice(start, start + columns) for start in range(0, LANES, columns)]
-    products = lax.dot_general(
-        stacked,
-        stacked,
-        (((0,), (0,)), ((), ())),
+    wraps = []
+    for wrap in range(0, len(chips), LANES // width):
+        rows_of_all = []
+        for second in range(2):
+            parts = [of_core(chip | core * second, second) for chip in chips[wrap : wrap + LANES // width]]
+            for chunk in range(2):
+                joined = moved(parts[0], chunk * half)
+                for number in range(1, len(parts)):
+                    here = moved(parts[number], (number * width + chunk * half) % LANES)
+                    joined = jnp.where(lane >= number * width, here, joined)
+                rows_of_all.append(joined)
+        wraps.append(jnp.concatenate(rows_of_all, axis=0))
+    sketch = jnp.concatenate(wraps, axis=1)
+    product = functools.partial(
+        lax.dot_general,
+        dimension_numbers=(((1,), (1,)), ((), ())),
         precision=lax.Precision.HIGHEST,
         preferred_element_type=jnp.float32,
     )
-    gram = sum([products[part, part] for part in parts[1:]], products[parts[0], parts[0]])
-    gram_ref[...] = gram * (1.0 / (count * 2 * rows))
-    own = of_chip(place_ref[0] & ~core)
-    on_first = place_ref[0] & core == 0
-    for half in range(2):
-        first, second = own[:, parts[half * 2]], own[:, parts[half * 2 + 1]]
-        sketch_ref[half * rows : (half + 1) * rows] = jnp.where(on_first, first, second)
+    gram_ref[...] = product(sketch, sketch) * (1.0 / (count * samples))
+    chip = place_ref[0] & ~core
+    own = []
+    for second in range(2):
+        part = of_core(chip | core * second, second)
+        own += [part, moved(part, half)]
+    start = jnp.where(place_ref[0] & core == 0, 0, samples)
+    row = lax.broadcasted_iota(jnp.int32, (samples, LANES), 0)
+    spot = lax.broadcasted_iota(jnp.int32, (samples, LANES), 1)
+    sketch_ref[...] = product(jnp.where(spot == row + start, 1.0, 0.0), jnp.concatenate(own, axis=0))
 
 
 def last_kernel(core, masks, place_ref, own_ref, other_ref, keep_ref, send_ref):
@@ -258,9 +266,8 @@
     shaped = jnp.einsum("cak,az->czk", shaped, table(outer), precision=lax.Precision.HIGHEST)
     current = shaped.reshape(columns, local_rows)
     for bit in range(count.bit_length() - 1):
-        other = exchange(current, 1, (1 << bit, 1 << bit))
-        lower = lax.axis_index(AXES) & 1 << bit == 0
-        current = jnp.where(lower, current + other, other - current)
+        masks = (1 << bit, 1 << bit)
+        current = combine(current, exchange(current, 1, masks), 1, masks)
     sketch = jnp.take(current, sample_offset, axis=1)
     gram = jnp.dot(sketch, sketch.T, precision=lax.Precision.HIGHEST)
     return (current, sketch, lax.psum(gram, AXES) / jnp.float32(samples * count))
@@ -281,8 +288,8 @@
     scaling = 1.0 / math.sqrt(local_rows * count)
     across = (core, core)
     orders = [
-        [(y, z_low), (x, z_high), (z_high, y), (z_low, x)],
-        [(x, z_high), (y, z_low), (z_low, x), (z_high, y)],
+        [(y, z_low), (z_low, y), (x, z_high), (z_high, x)],
+        [(x, z_high), (z_high, x), (y, z_low), (z_low, y)],
     ]
 
     other = exchange(matrix_slab, core, across)
@@ -309,39 +316,39 @@
     )
     ridden, thirds = [], []
     for current, order in zip(chunks, orders):
+        partner = exchange(current, core, order[0])
         current = call(
             functools.partial(mix_kernel, core, order[0]),
+            block(2 * ROWS, local_rows + LANES),
+            [IN_SMEM] + [IN_VMEM] * 3,
+            [place, current, partner, tile],
+        )
+        partner = exchange(current, core, order[1])
+        ridden.append(partner)
+        current = call(
+            functools.partial(step_kernel, core, order[1]),
             chunk,
             [IN_SMEM] + [IN_VMEM] * 2,
-            [place, current, exchange(current, core, order[0])],
+            [place, current, partner],
         )
-        current = call(
-            functools.partial(ride_kernel, core, order[1]),
-            block(2 * ROWS, local_rows + LANES),
-            [IN_SMEM] + [IN_VMEM] * 3,
-            [place, current, exchange(current, core, order[1]), tile],
-        )
-        partner = exchange(current, core, order[2])
-        ridden.append(partner)
-        thirds.append(
-            call(
-                functools.partial(step_kernel, core, order[2]),
-                chunk,
-                [IN_SMEM] + [IN_VMEM] * 2,
-                [place, current, partner],
-            )
-        )
-    first, second = thirds
+        thirds.append((current, exchange(current, core, order[2])))
     last_masks = [order[3] for order in orders]
+    second = combine(*thirds[1], core, orders[1][2])
     early = call(
         functools.partial(pick_kernel, core, samples, last_masks[1]),
         block(ROWS, LANES),
         [IN_SMEM] + [IN_VMEM] * 3,
         [place, tile, second, ridden[0]],
     )
+    first = call(
+        functools.partial(step_after_kernel, core, orders[0][2]),
+        chunk,
+        [IN_SMEM] + [IN_VMEM] * 3,
+        [place, *thirds[0], early],
+    )
     shares = call(
-        functools.partial(pick_all_kernel, core, last_masks[0]),
-        jax.ShapeDtypeStruct((count, samples // 2, LANES), jnp.float32),
+        functools.partial(pick_all_kernel, core, samples, last_masks[0]),
+        jax.ShapeDtypeStruct((count, ROWS, LANES), jnp.float32),
         [IN_SMEM] + [IN_VMEM] * 4,
         [place, tile, first, ridden[1], early],
     )

time: 46.1 us -> 45.5 us (0.987)
  waiting for transfers between devices: 19.7 us -> 18.4 us
  starting transfers between devices: 20.1 us -> 21 us
    ppermute x13, starting transfers between devices: 15.1 us -> 18.4 us  [exchange(): return lax.ppermute(array, AXES, route)]
    all_to_all x1, starting transfers between devices: 4.97 us -> 2.57 us  [local(): lax.all_to_all(shares, AXES, 0, 0, tiled=True)]
    all_to_all x1, waiting for transfers between devices: 2.95 us -> 1.72 us  [local(): lax.all_to_all(shares, AXES, 0, 0, tiled=True)]
    pallas_call x15 -> x14, Pallas kernels: 4.26 us -> 3.99 us  [call(): pl.pallas_call(body, out_shape=outputs, in_specs=in_specs, out_specs=jax....]
  transfers between devices with their start and end apart: 14 -> 14, of which waited for: 10 -> 8; matrix products, arithmetic and copies ran while one was open for 0% -> 0% of each run, Pallas kernels for 7% -> 6%
where the time goes in v3:
time: 45.5 us; the launch traced here: 45.2 us
  starting transfers between devices  21 us (46%)
  waiting for transfers between devices  18.4 us (40%)
  Pallas kernels  3.99 us (9%)
  local copies, waits for them, and re-layouts  1.05 us (2%)
  between operations  0.74 us (2%)
    ppermute x13, starting transfers between devices, exchange(): return lax.ppermute(array, AXES, route)  18.4 us
    ppermute x13, waiting for transfers between devices, exchange(): return lax.ppermute(array, AXES, route)  16.7 us
    pallas_call x14, Pallas kernels, call(): pl.pallas_call(body, out_shape=outputs, in_specs=in_specs, out_specs=jax....  3.99 us
    all_to_all x1, starting transfers between devices, local(): lax.all_to_all(shares, AXES, 0, 0, tiled=True)  2.57 us
    all_to_all x1, waiting for transfers between devices, local(): lax.all_to_all(shares, AXES, 0, 0, tiled=True)  1.72 us
    unnamed x6, local copies, waits for them, and re-layouts  1.05 us
  transfers between devices with their start and end apart: 14, of which 8 were waited for; matrix products, arithmetic and copies ran while one was open for 0% of the time, Pallas kernels for 6%

profile of v3, /device:TPU:0, one launch (start us, length us, event | category | flops | bytes accessed | tf_op | source)
XLA Modules:
  0.0 45.2 jit_solution(8640018184524744070)
XLA Ops:
  0.6 0.5 %collective-permute-start = (f32[32,4096]{1,0:T(8,128)}, f32[32,4096]{1,0:T(8,128)S(1)}, u32[]{:S(2)}, u32[]{:S(2)}) collective-permute-start(f32[32,4096]{1,0:T(8,128)} %slab_ref.1), channel_id=1, source_target_pairs={{0,8},{1,9},{2,10},{3,11},{4,12},{5,13},{6,14},{7,15},{8,0},{9,1},... | collective-permute-start | bytes 1572872 | tf_op jit(solution)/shard_map/ppermute | solution.py:41
  1.2 0.4 collective-permute-start.2
  1.7 1.0 %copy-done = f32[32,4096]{1,0:T(8,128)S(1)} copy-done((f32[32,4096]{1,0:T(8,128)S(1)}, f32[32,4096]{1,0:T(8,128)}, u32[]{:S(2)}) %copy-start) | copy-done | bytes 524312
  3.0 2.9 %collective-permute-start.6 = (f32[16,4096]{1,0:T(8,128)S(1)}, f32[16,4096]{1,0:T(8,128)S(1)}, u32[]{:S(2)}, u32[]{:S(2)}) collective-permute-start(f32[16,4096]{1,0:T(8,128)S(1)} %get-tuple-element.16.own_ref), channel_id=1, source_target_pairs={{0,16},{1,17},{2,18},{3,19},{4,20},{5,21},{6,22},{7,23},{8,12},{9,... | collective-permute-start | bytes 786440 | tf_op jit(solution)/shard_map/ppermute | solution.py:41
  6.0 1.5 %collective-permute-start.3 = (f32[16,4096]{1,0:T(8,128)S(1)}, f32[16,4096]{1,0:T(8,128)S(1)}, u32[]{:S(2)}, u32[]{:S(2)}) collective-permute-start(f32[16,4096]{1,0:T(8,128)S(1)} %get-tuple-element.14.own_ref), channel_id=1, source_target_pairs={{0,1},{1,0},{2,3},{3,2},{4,5},{5,4},{6,7},{7,6},{8,10},{9,11},{10,... | collective-permute-start | bytes 786440 | tf_op jit(solution)/shard_map/ppermute | solution.py:41
  7.6 2.7 %collective-permute-done.6.other_ref = f32[16,4096]{1,0:T(8,128)S(1)} collective-permute-done((f32[16,4096]{1,0:T(8,128)S(1)}, f32[16,4096]{1,0:T(8,128)S(1)}, u32[]{:S(2)}, u32[]{:S(2)}) %collective-permute-start.6) | collective-permute-done | bytes 262176 | tf_op jit(solution)/shard_map/ppermute | solution.py:41
  10.3 0.3 shard_map.63.own_ref
  10.6 3.2 %collective-permute-start.7 = (f32[16,4224]{1,0:T(8,128)S(1)}, f32[16,4224]{1,0:T(8,128)S(1)}, u32[]{:S(2)}, u32[]{:S(2)}) collective-permute-start(f32[16,4224]{1,0:T(8,128)S(1)} %shard_map.63.own_ref), channel_id=1, source_target_pairs={{0,4},{1,5},{2,6},{3,7},{4,0},{5,1},{6,2},{7,3},{8,24},{9,25},{10,... | collective-permute-start | bytes 811016 | tf_op jit(solution)/shard_map/ppermute | solution.py:41
  13.8 0.3 shard_map.61.own_ref
  14.1 1.6 %collective-permute-start.4 = (f32[16,4224]{1,0:T(8,128)S(1)}, f32[16,4224]{1,0:T(8,128)S(1)}, u32[]{:S(2)}, u32[]{:S(2)}) collective-permute-start(f32[16,4224]{1,0:T(8,128)S(1)} %shard_map.61.own_ref), channel_id=1, source_target_pairs={{0,2},{1,3},{2,0},{3,1},{4,6},{5,7},{6,4},{7,5},{8,9},{9,8},{10,11... | collective-permute-start | bytes 811016 | tf_op jit(solution)/shard_map/ppermute | solution.py:41
  15.8 5.5 %collective-permute-done.7.other_ref = f32[16,4224]{1,0:T(8,128)S(1)} collective-permute-done((f32[16,4224]{1,0:T(8,128)S(1)}, f32[16,4224]{1,0:T(8,128)S(1)}, u32[]{:S(2)}, u32[]{:S(2)}) %collective-permute-start.7) | collective-permute-done | bytes 270368 | tf_op jit(solution)/shard_map/ppermute | solution.py:41
  21.3 1.9 %collective-permute-start.8 = (f32[16,4096]{1,0:T(8,128)S(1)}, f32[16,4096]{1,0:T(8,128)S(1)}, u32[]{:S(2)}, u32[]{:S(2)}) collective-permute-start(f32[16,4096]{1,0:T(8,128)S(1)} %shard_map.64), channel_id=1, source_target_pairs={{0,1},{1,0},{2,3},{3,2},{4,5},{5,4},{6,7},{7,6},{8,10},{9,11},{10,... | collective-permute-start | bytes 786440 | tf_op jit(solution)/shard_map/ppermute | solution.py:41
  23.2 1.6 %collective-permute-start.5 = (f32[16,4096]{1,0:T(8,128)S(1)}, f32[16,4096]{1,0:T(8,128)S(1)}, u32[]{:S(2)}, u32[]{:S(2)}) collective-permute-start(f32[16,4096]{1,0:T(8,128)S(1)} %shard_map.62.own_ref), channel_id=1, source_target_pairs={{0,16},{1,17},{2,18},{3,19},{4,20},{5,21},{6,22},{7,23},{8,12},{9,... | collective-permute-start | bytes 786440 | tf_op jit(solution)/shard_map/ppermute | solution.py:41
  24.8 2.9 %collective-permute-done.8 = f32[16,4096]{1,0:T(8,128)S(1)} collective-permute-done((f32[16,4096]{1,0:T(8,128)S(1)}, f32[16,4096]{1,0:T(8,128)S(1)}, u32[]{:S(2)}, u32[]{:S(2)}) %collective-permute-start.8) | collective-permute-done | bytes 262176 | tf_op jit(solution)/shard_map/ppermute | solution.py:41
  27.7 1.0 %collective-permute-start.10 = (f32[16,4096]{1,0:T(8,128)S(1)}, f32[16,4096]{1,0:T(8,128)S(1)}, u32[]{:S(2)}, u32[]{:S(2)}) collective-permute-start(f32[16,4096]{1,0:T(8,128)S(1)} %subtract_select_fusion.chunk_ref.own_ref), channel_id=1, source_target_pairs={{0,2},{1,3},{2,0},{3,1},{4,6},{5,7},{6,4},{7,5},{8,9},{9,8},{10,11... | collective-permute-start | bytes 786440 | tf_op jit(solution)/shard_map/ppermute | solution.py:41
  29.0 0.6 %collective-permute-done.5.other_ref = f32[16,4096]{1,0:T(8,128)S(1)} collective-permute-done((f32[16,4096]{1,0:T(8,128)S(1)}, f32[16,4096]{1,0:T(8,128)S(1)}, u32[]{:S(2)}, u32[]{:S(2)}) %collective-permute-start.5) | collective-permute-done | bytes 262176 | tf_op jit(solution)/shard_map/ppermute | solution.py:41
  29.7 3.3 %collective-permute-start.9 = (f32[16,4096]{1,0:T(8,128)S(1)}, f32[16,4096]{1,0:T(8,128)S(1)}, u32[]{:S(2)}, u32[]{:S(2)}) collective-permute-start(f32[16,4096]{1,0:T(8,128)S(1)} %shard_map.66.own_ref.chunk_ref), channel_id=1, source_target_pairs={{0,4},{1,5},{2,6},{3,7},{4,0},{5,1},{6,2},{7,3},{8,24},{9,25},{10,... | collective-permute-start | bytes 786440 | tf_op jit(solution)/shard_map/ppermute | solution.py:41
  33.0 0.9 %shard_map.70 = f32[32,8,128]{2,1,0:T(8,128)} custom-call(s32[1]{0:T(128)} %bitcast.place_ref, f32[8,128]{1,0:T(8,128)S(1)} %shard_map.60.tile_ref, f32[16,4096]{1,0:T(8,128)S(1)} %shard_map.66.own_ref.chunk_ref, f32[16,4224]{1,0:T(8,128)S(1)} %collective-permute-done.7.other_ref, f32[8,128]{1,0:T(8,128)S(1)} %shard_map.65.after_ref.early_ref), custom_call_target="tpu_custom_call" | custom-call | tf_op jit(solution)/shard_map/pallas_call | solution.py:20
  33.9 2.6 %all-to-all-start = ((f32[32,8,128]{2,1,0:T(8,128)}), f32[32,8,128]{2,1,0:T(8,128)S(1)}, u32[]{:S(2)}, u32[]{:S(2)}) async-start(f32[32,8,128]{2,1,0:T(8,128)} %shard_map.70), calls=%async_computation | async-start | bytes 262144 | tf_op jit(solution)/shard_map/all_to_all | solution.py:378
  36.8 3.4 %collective-permute-done.9.other_ref = f32[16,4096]{1,0:T(8,128)S(1)} collective-permute-done((f32[16,4096]{1,0:T(8,128)S(1)}, f32[16,4096]{1,0:T(8,128)S(1)}, u32[]{:S(2)}, u32[]{:S(2)}) %collective-permute-start.9) | collective-permute-done | bytes 262176 | tf_op jit(solution)/shard_map/ppermute | solution.py:41
  40.4 1.3 %collective-permute-done.11.refs_2_ = f32[8,4096]{1,0:T(8,128)S(1)} collective-permute-done((f32[8,4096]{1,0:T(8,128)S(1)}, f32[8,4096]{1,0:T(8,128)S(1)}, u32[]{:S(2)}, u32[]{:S(2)}) %collective-permute-start.11) | collective-permute-done | bytes 131104 | tf_op jit(solution)/shard_map/ppermute | solution.py:41
  41.7 0.8 %shard_map.69 = (f32[32,4096]{1,0:T(8,128)}, f32[8,128]{1,0:T(8,128)S(1)}) custom-call(s32[1]{0:T(128)} %bitcast.place_ref, f32[8,4096]{1,0:T(8,128)S(1)} %get-tuple-element.17.refs_0_, f32[8,4096]{1,0:T(8,128)S(1)} %get-tuple-element.18.refs_1_, f32[8,4096]{1,0:T(8,128)S(1)} %collective-permute-done.11.refs_2_, f32[8,4096]{1,0:T(8,128)S(1)} %collective-permute-done.12.refs_3_), custom_call_target="tpu_custom_call" | custom-call | tf_op jit(solution)/shard_map/pallas_call | solution.py:20
  42.5 1.7 %all-to-all-done.shares_ref = f32[32,8,128]{2,1,0:T(8,128)S(1)} async-done(((f32[32,8,128]{2,1,0:T(8,128)}), f32[32,8,128]{2,1,0:T(8,128)S(1)}, u32[]{:S(2)}, u32[]{:S(2)}) %all-to-all-start) | async-done | bytes 131104 | tf_op jit(solution)/shard_map/all_to_all | solution.py:378
  44.2 1.0 %shard_map.71 = (f32[32,32]{1,0:T(8,128)}, f32[16,32]{1,0:T(8,128)}) custom-call(s32[1]{0:T(128)} %bitcast.place_ref, f32[32,8,128]{2,1,0:T(8,128)S(1)} %all-to-all-done.shares_ref, f32[8,128]{1,0:T(8,128)S(1)} %get-tuple-element.22.after_ref), custom_call_target="tpu_custom_call" | custom-call | tf_op jit(solution)/shard_map/pallas_call | solution.py:20
  (25 shorter events, 1.3 us)
Async XLA Ops:
  0.6 1.0 %copy-start.1 = (s32[4096]{0:T(1024)S(1)}, s32[4096]{0:T(1024)}, u32[]{:S(2)}) copy-start(s32[4096]{0:T(1024)} %param.4) | copy-start | bytes 49156
  0.6 2.3 %collective-permute-start = (f32[32,4096]{1,0:T(8,128)}, f32[32,4096]{1,0:T(8,128)S(1)}, u32[]{:S(2)}, u32[]{:S(2)}) collective-permute-start(f32[32,4096]{1,0:T(8,128)} %slab_ref.1), channel_id=1, source_target_pairs={{0,8},{1,9},{2,10},{3,11},{4,12},{5,13},{6,14},{7,15},{8,0},{9,1},... | collective-permute-start | bytes 1572872 | tf_op jit(solution)/shard_map/ppermute | solution.py:41
  1.2 1.8 %collective-permute-start.1 = (s32[32,128]{1,0:T(8,128)}, s32[32,128]{1,0:T(8,128)S(1)}, u32[]{:S(2)}, u32[]{:S(2)}) collective-permute-start(s32[32,128]{1,0:T(8,128)} %bitcast.4), channel_id=1, source_target_pairs={{0,8},{1,9},{2,10},{3,11},{4,12},{5,13},{6,14},{7,15},{8,0},{9,1},... | collective-permute-start | bytes 49160 | tf_op jit(solution)/shard_map/ppermute | solution.py:41
  1.2 1.7 %collective-permute-start.2 = (s32[1,16]{1,0:T(1,128)}, s32[1,16]{1,0:T(1,128)S(1)}, u32[]{:S(2)}, u32[]{:S(2)}) collective-permute-start(s32[1,16]{1,0:T(1,128)} %bitcast.6), channel_id=1, source_target_pairs={{0,8},{1,9},{2,10},{3,11},{4,12},{5,13},{6,14},{7,15},{8,0},{9,1},... | collective-permute-start | bytes 200 | tf_op jit(solution)/shard_map/ppermute | solution.py:41
  1.7 1.0 %copy-start = (f32[32,4096]{1,0:T(8,128)S(1)}, f32[32,4096]{1,0:T(8,128)}, u32[]{:S(2)}) copy-start(f32[32,4096]{1,0:T(8,128)} %slab_ref.1) | copy-start | bytes 1572868
  3.0 2.9 %copy-start.2 = (s32[16]{0:T(128)S(1)}, s32[16]{0:T(128)}, u32[]{:S(2)}) copy-start(s32[16]{0:T(128)} %param.5) | copy-start | bytes 196
  3.0 7.3 %collective-permute-start.6 = (f32[16,4096]{1,0:T(8,128)S(1)}, f32[16,4096]{1,0:T(8,128)S(1)}, u32[]{:S(2)}, u32[]{:S(2)}) collective-permute-start(f32[16,4096]{1,0:T(8,128)S(1)} %get-tuple-element.16.own_ref), channel_id=1, source_target_pairs={{0,16},{1,17},{2,18},{3,19},{4,20},{5,21},{6,22},{7,23},{8,12},{9,... | collective-permute-start | bytes 786440 | tf_op jit(solution)/shard_map/ppermute | solution.py:41
  6.0 7.8 %collective-permute-start.3 = (f32[16,4096]{1,0:T(8,128)S(1)}, f32[16,4096]{1,0:T(8,128)S(1)}, u32[]{:S(2)}, u32[]{:S(2)}) collective-permute-start(f32[16,4096]{1,0:T(8,128)S(1)} %get-tuple-element.14.own_ref), channel_id=1, source_target_pairs={{0,1},{1,0},{2,3},{3,2},{4,5},{5,4},{6,7},{7,6},{8,10},{9,11},{10,... | collective-permute-start | bytes 786440 | tf_op jit(solution)/shard_map/ppermute | solution.py:41
  10.6 10.6 %collective-permute-start.7 = (f32[16,4224]{1,0:T(8,128)S(1)}, f32[16,4224]{1,0:T(8,128)S(1)}, u32[]{:S(2)}, u32[]{:S(2)}) collective-permute-start(f32[16,4224]{1,0:T(8,128)S(1)} %shard_map.63.own_ref), channel_id=1, source_target_pairs={{0,4},{1,5},{2,6},{3,7},{4,0},{5,1},{6,2},{7,3},{8,24},{9,25},{10,... | collective-permute-start | bytes 811016 | tf_op jit(solution)/shard_map/ppermute | solution.py:41
  14.1 9.1 %collective-permute-start.4 = (f32[16,4224]{1,0:T(8,128)S(1)}, f32[16,4224]{1,0:T(8,128)S(1)}, u32[]{:S(2)}, u32[]{:S(2)}) collective-permute-start(f32[16,4224]{1,0:T(8,128)S(1)} %shard_map.61.own_ref), channel_id=1, source_target_pairs={{0,2},{1,3},{2,0},{3,1},{4,6},{5,7},{6,4},{7,5},{8,9},{9,8},{10,11... | collective-permute-start | bytes 811016 | tf_op jit(solution)/shard_map/ppermute | solution.py:41
  21.3 6.4 %collective-permute-start.8 = (f32[16,4096]{1,0:T(8,128)S(1)}, f32[16,4096]{1,0:T(8,128)S(1)}, u32[]{:S(2)}, u32[]{:S(2)}) collective-permute-start(f32[16,4096]{1,0:T(8,128)S(1)} %shard_map.64), channel_id=1, source_target_pairs={{0,1},{1,0},{2,3},{3,2},{4,5},{5,4},{6,7},{7,6},{8,10},{9,11},{10,... | collective-permute-start | bytes 786440 | tf_op jit(solution)/shard_map/ppermute | solution.py:41
  23.2 6.4 %collective-permute-start.5 = (f32[16,4096]{1,0:T(8,128)S(1)}, f32[16,4096]{1,0:T(8,128)S(1)}, u32[]{:S(2)}, u32[]{:S(2)}) collective-permute-start(f32[16,4096]{1,0:T(8,128)S(1)} %shard_map.62.own_ref), channel_id=1, source_target_pairs={{0,16},{1,17},{2,18},{3,19},{4,20},{5,21},{6,22},{7,23},{8,12},{9,... | collective-permute-start | bytes 786440 | tf_op jit(solution)/shard_map/ppermute | solution.py:41
  27.7 8.8 %collective-permute-start.10 = (f32[16,4096]{1,0:T(8,128)S(1)}, f32[16,4096]{1,0:T(8,128)S(1)}, u32[]{:S(2)}, u32[]{:S(2)}) collective-permute-start(f32[16,4096]{1,0:T(8,128)S(1)} %subtract_select_fusion.chunk_ref.own_ref), channel_id=1, source_target_pairs={{0,2},{1,3},{2,0},{3,1},{4,6},{5,7},{6,4},{7,5},{8,9},{9,8},{10,11... | collective-permute-start | bytes 786440 | tf_op jit(solution)/shard_map/ppermute | solution.py:41
  29.7 10.5 %collective-permute-start.9 = (f32[16,4096]{1,0:T(8,128)S(1)}, f32[16,4096]{1,0:T(8,128)S(1)}, u32[]{:S(2)}, u32[]{:S(2)}) collective-permute-start(f32[16,4096]{1,0:T(8,128)S(1)} %shard_map.66.own_ref.chunk_ref), channel_id=1, source_target_pairs={{0,4},{1,5},{2,6},{3,7},{4,0},{5,1},{6,2},{7,3},{8,24},{9,25},{10,... | collective-permute-start | bytes 786440 | tf_op jit(solution)/shard_map/ppermute | solution.py:41
  33.9 10.3 %all-to-all-start = ((f32[32,8,128]{2,1,0:T(8,128)}), f32[32,8,128]{2,1,0:T(8,128)S(1)}, u32[]{:S(2)}, u32[]{:S(2)}) async-start(f32[32,8,128]{2,1,0:T(8,128)} %shard_map.70), calls=%async_computation | async-start | bytes 262144 | tf_op jit(solution)/shard_map/all_to_all | solution.py:378
  36.6 3.8 %collective-permute-start.12 = (f32[8,4096]{1,0:T(8,128)S(1)}, f32[8,4096]{1,0:T(8,128)S(1)}, u32[]{:S(2)}, u32[]{:S(2)}) collective-permute-start(f32[8,4096]{1,0:T(8,128)S(1)} %get-tuple-element.20), channel_id=1, source_target_pairs={{0,8},{1,9},{2,10},{3,11},{4,12},{5,13},{6,14},{7,15},{8,0},{9,1},... | collective-permute-start | bytes 393224 | tf_op jit(solution)/shard_map/ppermute | solution.py:41
  40.3 1.4 %collective-permute-start.11 = (f32[8,4096]{1,0:T(8,128)S(1)}, f32[8,4096]{1,0:T(8,128)S(1)}, u32[]{:S(2)}, u32[]{:S(2)}) collective-permute-start(f32[8,4096]{1,0:T(8,128)S(1)} %get-tuple-element.19), channel_id=1, source_target_pairs={{0,8},{1,9},{2,10},{3,11},{4,12},{5,13},{6,14},{7,15},{8,0},{9,1},... | collective-permute-start | bytes 393224 | tf_op jit(solution)/shard_map/ppermute | solution.py:41

commit v4 on v3

--- a/solution.py
+++ b/solution.py
@@ -67,13 +67,17 @@
     return total
 
 
+def sign_of(left, right):
+    parity = left & right
+    for shift in (4, 2, 1):
+        parity = parity ^ (parity >> shift)
+    return (1 - 2 * (parity & 1)).astype(jnp.float32)
+
+
 def mix(parts):
     left = lax.broadcasted_iota(jnp.int32, (LANES, LANES), 0)
     right = lax.broadcasted_iota(jnp.int32, (LANES, LANES), 1)
-    parity = left & right
-    for shift in (4, 2, 1):
-        parity = parity ^ (parity >> shift)
-    table = (1 - 2 * (parity & 1)).astype(jnp.float32).astype(jnp.bfloat16)
+    table = sign_of(left, right).astype(jnp.bfloat16)
     parts = list(parts)
     span = 1
     while span < len(parts):
@@ -122,16 +126,12 @@
     tile_ref[...] = jnp.broadcast_to(tile.astype(jnp.float32), tile_ref.shape)
 
 
-def mix_kernel(core, masks, place_ref, own_ref, other_ref, tile_ref, out_ref):
-    slices = own_ref.shape[1] // LANES
+def ride_kernel(core, masks, place_ref, own_ref, other_ref, tile_ref, out_ref):
+    width = own_ref.shape[1]
     factor = jnp.where(place_ref[0] & chosen_mask(place_ref[0], core, masks) == 0, 1.0, -1.0)
-    parts = [
-        own_ref[:, lanes_of(index)] * factor + other_ref[:, lanes_of(index)] for index in range(slices)
-    ]
-    for index, part in enumerate(mix(parts)):
-        out_ref[:, lanes_of(index)] = part
+    out_ref[:, :width] = own_ref[...] * factor + other_ref[...]
     for row in range(0, own_ref.shape[0], ROWS):
-        out_ref[row : row + ROWS, lanes_of(slices)] = tile_ref[...]
+        out_ref[row : row + ROWS, width:] = tile_ref[...]
 
 
 def step_kernel(core, masks, place_ref, own_ref, other_ref, out_ref):
@@ -150,15 +150,15 @@
     own_chip = lane < 2 * samples
     partner = other_ref[0:1, other_ref.shape[1] - LANES :]
     offsets = jnp.where(own_chip, tile_ref[0:1, :], partner).astype(jnp.int32)
-    chosen = jnp.where(place_in == offsets % LANES, 1.0, 0.0).astype(jnp.bfloat16)
+    signs = sign_of(place_in, offsets % LANES).astype(jnp.bfloat16)
     side = jnp.where(place_ref[0] & chosen_mask(place_ref[0], core, masks) == 0, 1.0, -1.0)
     slices = chunk_ref.shape[1] // LANES
     rows = chunk_ref.shape[0]
     stacked = jnp.concatenate([chunk_ref[:, lanes_of(index)] for index in range(slices)], axis=0)
-    found = exact_dot(stacked, chosen)
-    share = jnp.zeros((rows, LANES), jnp.float32)
-    for index in range(slices):
-        share = jnp.where(offsets // LANES == index, found[index * rows : (index + 1) * rows], share)
+    found = exact_dot(stacked, signs)
+    share = found[:rows]
+    for index in range(1, slices):
+        share = share + found[index * rows : (index + 1) * rows] * sign_of(offsets // LANES, index)
     share = jnp.where(lane // samples % 2 == 0, share[:ROWS], share[ROWS:])
     return share * jnp.where(own_chip, side, 1.0)
 
@@ -167,7 +167,8 @@
     out_ref[...] = pick(core, samples, masks, place_ref, tile_ref, chunk_ref, other_ref)
 
 
-def pick_all_kernel(core, samples, masks, place_ref, tile_ref, chunk_ref, other_ref, early_ref, out_ref):
+def pick_all_kernel(core, samples, masks, place_ref, tile_ref, chunk_ref, other_ref, early_ref, out_ref, token_ref):
+    token_ref[...] = jnp.zeros_like(token_ref)
     late = pick(core, samples, masks, place_ref, tile_ref, chunk_ref, other_ref)
     lane = lax.broadcasted_iota(jnp.int32, late.shape, 1)
     tile = jnp.where(lane < LANES // 2, late, pltpu.roll(early_ref[...], LANES // 2, 1))
@@ -220,12 +221,17 @@
     sketch_ref[...] = product(jnp.where(spot == row + start, 1.0, 0.0), jnp.concatenate(own, axis=0))
 
 
-def last_kernel(core, masks, place_ref, own_ref, other_ref, keep_ref, send_ref):
+def last_kernel(core, masks, place_ref, own_ref, other_ref, after_ref, keep_ref, send_ref):
     on_first = place_ref[0] & core == 0
     factor = jnp.where(place_ref[0] & chosen_mask(place_ref[0], core, masks) == 0, 1.0, -1.0)
     for out_ref, top in ((keep_ref, jnp.where(on_first, 0, ROWS)), (send_ref, jnp.where(on_first, ROWS, 0))):
         rows = pl.ds(pl.multiple_of(top, ROWS), ROWS)
-        out_ref[...] = own_ref[rows, :] * factor + other_ref[rows, :]
+        slices = out_ref.shape[1] // LANES
+        parts = [
+            own_ref[rows, lanes_of(index)] * factor + other_ref[rows, lanes_of(index)] for index in range(slices)
+        ]
+        for index, part in enumerate(mix(parts)):
+            out_ref[:, lanes_of(index)] = part
 
 
 def join_kernel(core, place_ref, *refs):
@@ -318,7 +324,7 @@
     for current, order in zip(chunks, orders):
         partner = exchange(current, core, order[0])
         current = call(
-            functools.partial(mix_kernel, core, order[0]),
+            functools.partial(ride_kernel, core, order[0]),
             block(2 * ROWS, local_rows + LANES),
             [IN_SMEM] + [IN_VMEM] * 3,
             [place, current, partner, tile],
@@ -346,21 +352,34 @@
         [IN_SMEM] + [IN_VMEM] * 3,
         [place, *thirds[0], early],
     )
-    shares = call(
+    shares, picked = call(
         functools.partial(pick_all_kernel, core, samples, last_masks[0]),
-        jax.ShapeDtypeStruct((count, ROWS, LANES), jnp.float32),
+        [jax.ShapeDtypeStruct((count, ROWS, LANES), jnp.float32), block(ROWS, LANES)],
         [IN_SMEM] + [IN_VMEM] * 4,
         [place, tile, first, ridden[1], early],
     )
+    later = call(
+        functools.partial(step_after_kernel, core, orders[1][2]),
+        chunk,
+        [IN_SMEM] + [IN_VMEM] * 3,
+        [place, *thirds[1], picked],
+    )
     lasts = [
         call(
-            functools.partial(last_kernel, core, masks),
+            functools.partial(last_kernel, core, last_masks[0]),
             [block(ROWS, local_rows)] * 2,
-            [IN_SMEM] + [IN_VMEM] * 2,
-            [place, current, exchange(current, core, masks)],
+            [IN_SMEM] + [IN_VMEM] * 3,
+            [place, first, exchange(first, core, last_masks[0]), picked],
         )
-        for current, masks in zip((first, second), last_masks)
     ]
+    lasts.append(
+        call(
+            functools.partial(last_kernel, core, last_masks[1]),
+            [block(ROWS, local_rows)] * 2,
+            [IN_SMEM] + [IN_VMEM] * 3,
+            [place, later, exchange(later, core, last_masks[1]), lasts[0][0]],
+        )
+    )
     kept = [keep for keep, _ in lasts]
     back = [exchange(send, core, across) for _, send in lasts]
     transformed, token = call(

time: 45.5 us -> 46.1 us (1.013)
  waiting for transfers between devices: 18.4 us -> 18.9 us
    ppermute x13, waiting for transfers between devices: 16.7 us -> 18.6 us  [exchange(): return lax.ppermute(array, AXES, route)]
    all_to_all x1, waiting for transfers between devices: 1.72 us -> 0.27 us  [local(): lax.all_to_all(shares, AXES, 0, 0, tiled=True)]
    pallas_call x14 -> x15, Pallas kernels: 3.99 us -> 4.1 us  [call(): pl.pallas_call(body, out_shape=outputs, in_specs=in_specs, out_specs=jax....]
  transfers between devices with their start and end apart: 14 -> 14, of which waited for: 8 -> 10; matrix products, arithmetic and copies ran while one was open for 0% -> 0% of each run, Pallas kernels for 6% -> 7%
where the time goes in v4:
time: 46.1 us; the launch traced here: 45.9 us
  starting transfers between devices  21.1 us (46%)
  waiting for transfers between devices  18.9 us (41%)
  Pallas kernels  4.1 us (9%)
  local copies, waits for them, and re-layouts  1.05 us (2%)
  between operations  0.72 us (2%)
    ppermute x13, waiting for transfers between devices, exchange(): return lax.ppermute(array, AXES, route)  18.6 us
    ppermute x13, starting transfers between devices, exchange(): return lax.ppermute(array, AXES, route)  18.5 us
    pallas_call x15, Pallas kernels, call(): pl.pallas_call(body, out_shape=outputs, in_specs=in_specs, out_specs=jax....  4.1 us
    all_to_all x1, starting transfers between devices, local(): lax.all_to_all(shares, AXES, 0, 0, tiled=True)  2.56 us
    unnamed x6, local copies, waits for them, and re-layouts  1.05 us
  transfers between devices with their start and end apart: 14, of which 10 were waited for; matrix products, arithmetic and copies ran while one was open for 0% of the time, Pallas kernels for 7%

profile of v4, /device:TPU:0, one launch (start us, length us, event | category | flops | bytes accessed | tf_op | source)
XLA Modules:
  0.0 45.9 jit_solution(5844316984841817648)
XLA Ops:
  0.6 0.5 %collective-permute-start = (f32[32,4096]{1,0:T(8,128)}, f32[32,4096]{1,0:T(8,128)S(1)}, u32[]{:S(2)}, u32[]{:S(2)}) collective-permute-start(f32[32,4096]{1,0:T(8,128)} %slab_ref.1), channel_id=1, source_target_pairs={{0,8},{1,9},{2,10},{3,11},{4,12},{5,13},{6,14},{7,15},{8,0},{9,1},... | collective-permute-start | bytes 1572872 | tf_op jit(solution)/shard_map/ppermute | solution.py:41
  1.2 0.4 collective-permute-start.2
  1.7 1.0 %copy-done = f32[32,4096]{1,0:T(8,128)S(1)} copy-done((f32[32,4096]{1,0:T(8,128)S(1)}, f32[32,4096]{1,0:T(8,128)}, u32[]{:S(2)}) %copy-start) | copy-done | bytes 524312
  3.0 2.9 %collective-permute-start.6 = (f32[16,4096]{1,0:T(8,128)S(1)}, f32[16,4096]{1,0:T(8,128)S(1)}, u32[]{:S(2)}, u32[]{:S(2)}) collective-permute-start(f32[16,4096]{1,0:T(8,128)S(1)} %get-tuple-element.18.own_ref), channel_id=1, source_target_pairs={{0,16},{1,17},{2,18},{3,19},{4,20},{5,21},{6,22},{7,23},{8,12},{9,... | collective-permute-start | bytes 786440 | tf_op jit(solution)/shard_map/ppermute | solution.py:41
  6.0 1.5 %collective-permute-start.3 = (f32[16,4096]{1,0:T(8,128)S(1)}, f32[16,4096]{1,0:T(8,128)S(1)}, u32[]{:S(2)}, u32[]{:S(2)}) collective-permute-start(f32[16,4096]{1,0:T(8,128)S(1)} %get-tuple-element.16.own_ref), channel_id=1, source_target_pairs={{0,1},{1,0},{2,3},{3,2},{4,5},{5,4},{6,7},{7,6},{8,10},{9,11},{10,... | collective-permute-start | bytes 786440 | tf_op jit(solution)/shard_map/ppermute | solution.py:41
  7.6 2.7 %collective-permute-done.6.other_ref = f32[16,4096]{1,0:T(8,128)S(1)} collective-permute-done((f32[16,4096]{1,0:T(8,128)S(1)}, f32[16,4096]{1,0:T(8,128)S(1)}, u32[]{:S(2)}, u32[]{:S(2)}) %collective-permute-start.6) | collective-permute-done | bytes 262176 | tf_op jit(solution)/shard_map/ppermute | solution.py:41
  10.3 3.2 %collective-permute-start.7 = (f32[16,4224]{1,0:T(8,128)S(1)}, f32[16,4224]{1,0:T(8,128)S(1)}, u32[]{:S(2)}, u32[]{:S(2)}) collective-permute-start(f32[16,4224]{1,0:T(8,128)S(1)} %shard_map.63.own_ref), channel_id=1, source_target_pairs={{0,4},{1,5},{2,6},{3,7},{4,0},{5,1},{6,2},{7,3},{8,24},{9,25},{10,... | collective-permute-start | bytes 811016 | tf_op jit(solution)/shard_map/ppermute | solution.py:41
  13.5 1.6 %collective-permute-start.4 = (f32[16,4224]{1,0:T(8,128)S(1)}, f32[16,4224]{1,0:T(8,128)S(1)}, u32[]{:S(2)}, u32[]{:S(2)}) collective-permute-start(f32[16,4224]{1,0:T(8,128)S(1)} %shard_map.61.own_ref), channel_id=1, source_target_pairs={{0,2},{1,3},{2,0},{3,1},{4,6},{5,7},{6,4},{7,5},{8,9},{9,8},{10,11... | collective-permute-start | bytes 811016 | tf_op jit(solution)/shard_map/ppermute | solution.py:41
  15.2 5.8 %collective-permute-done.7.other_ref = f32[16,4224]{1,0:T(8,128)S(1)} collective-permute-done((f32[16,4224]{1,0:T(8,128)S(1)}, f32[16,4224]{1,0:T(8,128)S(1)}, u32[]{:S(2)}, u32[]{:S(2)}) %collective-permute-start.7) | collective-permute-done | bytes 270368 | tf_op jit(solution)/shard_map/ppermute | solution.py:41
  21.0 1.9 %collective-permute-start.8 = (f32[16,4096]{1,0:T(8,128)S(1)}, f32[16,4096]{1,0:T(8,128)S(1)}, u32[]{:S(2)}, u32[]{:S(2)}) collective-permute-start(f32[16,4096]{1,0:T(8,128)S(1)} %shard_map.64.own_ref), channel_id=1, source_target_pairs={{0,1},{1,0},{2,3},{3,2},{4,5},{5,4},{6,7},{7,6},{8,10},{9,11},{10,... | collective-permute-start | bytes 786440 | tf_op jit(solution)/shard_map/ppermute | solution.py:41
  23.0 1.6 %collective-permute-start.5 = (f32[16,4096]{1,0:T(8,128)S(1)}, f32[16,4096]{1,0:T(8,128)S(1)}, u32[]{:S(2)}, u32[]{:S(2)}) collective-permute-start(f32[16,4096]{1,0:T(8,128)S(1)} %shard_map.62.own_ref), channel_id=1, source_target_pairs={{0,16},{1,17},{2,18},{3,19},{4,20},{5,21},{6,22},{7,23},{8,12},{9,... | collective-permute-start | bytes 786440 | tf_op jit(solution)/shard_map/ppermute | solution.py:41
  24.5 2.9 %collective-permute-done.8.other_ref = f32[16,4096]{1,0:T(8,128)S(1)} collective-permute-done((f32[16,4096]{1,0:T(8,128)S(1)}, f32[16,4096]{1,0:T(8,128)S(1)}, u32[]{:S(2)}, u32[]{:S(2)}) %collective-permute-start.8) | collective-permute-done | bytes 262176 | tf_op jit(solution)/shard_map/ppermute | solution.py:41
  27.8 1.6 %collective-permute-done.5.other_ref = f32[16,4096]{1,0:T(8,128)S(1)} collective-permute-done((f32[16,4096]{1,0:T(8,128)S(1)}, f32[16,4096]{1,0:T(8,128)S(1)}, u32[]{:S(2)}, u32[]{:S(2)}) %collective-permute-start.5) | collective-permute-done | bytes 262176 | tf_op jit(solution)/shard_map/ppermute | solution.py:41
  29.4 0.6 %collective-permute-start.9 = (f32[16,4096]{1,0:T(8,128)S(1)}, f32[16,4096]{1,0:T(8,128)S(1)}, u32[]{:S(2)}, u32[]{:S(2)}) collective-permute-start(f32[16,4096]{1,0:T(8,128)S(1)} %shard_map.66.chunk_ref.own_ref), channel_id=1, source_target_pairs={{0,4},{1,5},{2,6},{3,7},{4,0},{5,1},{6,2},{7,3},{8,24},{9,25},{10,... | collective-permute-start | bytes 786440 | tf_op jit(solution)/shard_map/ppermute | solution.py:41
  30.1 1.0 %shard_map.67 = (f32[32,8,128]{2,1,0:T(8,128)}, f32[8,128]{1,0:T(8,128)S(1)}) custom-call(s32[1]{0:T(128)} %bitcast.place_ref, f32[8,128]{1,0:T(8,128)S(1)} %shard_map.60.tile_ref, f32[16,4096]{1,0:T(8,128)S(1)} %shard_map.66.chunk_ref.own_ref, f32[16,4224]{1,0:T(8,128)S(1)} %collective-permute-done.7.other_ref, f32[8,128]{1,0:T(8,128)S(1)} %shard_map.65.after_ref.early_ref), custom_call_target="tpu_custom_call" | custom-call | tf_op jit(solution)/shard_map/pallas_call | solution.py:20
  31.1 3.5 %collective-permute-start.10 = (f32[16,4096]{1,0:T(8,128)S(1)}, f32[16,4096]{1,0:T(8,128)S(1)}, u32[]{:S(2)}, u32[]{:S(2)}) collective-permute-start(f32[16,4096]{1,0:T(8,128)S(1)} %shard_map.69.own_ref), channel_id=1, source_target_pairs={{0,2},{1,3},{2,0},{3,1},{4,6},{5,7},{6,4},{7,5},{8,9},{9,8},{10,11... | collective-permute-start | bytes 786440 | tf_op jit(solution)/shard_map/ppermute | solution.py:41
  34.6 2.6 %all-to-all-start = ((f32[32,8,128]{2,1,0:T(8,128)}), f32[32,8,128]{2,1,0:T(8,128)S(1)}, u32[]{:S(2)}, u32[]{:S(2)}) async-start(f32[32,8,128]{2,1,0:T(8,128)} %get-tuple-element.25), calls=%async_computation | async-start | bytes 262144 | tf_op jit(solution)/shard_map/all_to_all | solution.py:397
  37.2 2.5 %collective-permute-done.9.other_ref = f32[16,4096]{1,0:T(8,128)S(1)} collective-permute-done((f32[16,4096]{1,0:T(8,128)S(1)}, f32[16,4096]{1,0:T(8,128)S(1)}, u32[]{:S(2)}, u32[]{:S(2)}) %collective-permute-start.9) | collective-permute-done | bytes 262176 | tf_op jit(solution)/shard_map/ppermute | solution.py:41
  39.7 0.3 shard_map.68
  40.0 1.9 %collective-permute-done.10.other_ref = f32[16,4096]{1,0:T(8,128)S(1)} collective-permute-done((f32[16,4096]{1,0:T(8,128)S(1)}, f32[16,4096]{1,0:T(8,128)S(1)}, u32[]{:S(2)}, u32[]{:S(2)}) %collective-permute-start.10) | collective-permute-done | bytes 262176 | tf_op jit(solution)/shard_map/ppermute | solution.py:41
  42.3 0.5 %collective-permute-start.11 = (f32[8,4096]{1,0:T(8,128)S(1)}, f32[8,4096]{1,0:T(8,128)S(1)}, u32[]{:S(2)}, u32[]{:S(2)}) collective-permute-start(f32[8,4096]{1,0:T(8,128)S(1)} %get-tuple-element.22), channel_id=1, source_target_pairs={{0,8},{1,9},{2,10},{3,11},{4,12},{5,13},{6,14},{7,15},{8,0},{9,1},... | collective-permute-start | bytes 393224 | tf_op jit(solution)/shard_map/ppermute | solution.py:41
  42.8 0.8 %collective-permute-done.12.refs_3_ = f32[8,4096]{1,0:T(8,128)S(1)} collective-permute-done((f32[8,4096]{1,0:T(8,128)S(1)}, f32[8,4096]{1,0:T(8,128)S(1)}, u32[]{:S(2)}, u32[]{:S(2)}) %collective-permute-start.12) | collective-permute-done | bytes 131104 | tf_op jit(solution)/shard_map/ppermute | solution.py:41
  43.8 0.8 %shard_map.71 = (f32[32,4096]{1,0:T(8,128)}, f32[8,128]{1,0:T(8,128)S(1)}) custom-call(s32[1]{0:T(128)} %bitcast.place_ref, f32[8,4096]{1,0:T(8,128)S(1)} %get-tuple-element.20.after_ref.refs_0_, f32[8,4096]{1,0:T(8,128)S(1)} %get-tuple-element.21.refs_1_, f32[8,4096]{1,0:T(8,128)S(1)} %collective-permute-done.11.refs_2_, ...), custom_call_target="tpu_custom_call" | custom-call | tf_op jit(solution)/shard_map/pallas_call | solution.py:20
  44.9 1.0 %shard_map.72 = (f32[32,32]{1,0:T(8,128)}, f32[16,32]{1,0:T(8,128)}) custom-call(s32[1]{0:T(128)} %bitcast.place_ref, f32[32,8,128]{2,1,0:T(8,128)S(1)} %all-to-all-done.shares_ref, f32[8,128]{1,0:T(8,128)S(1)} %get-tuple-element.26.after_ref), custom_call_target="tpu_custom_call" | custom-call | tf_op jit(solution)/shard_map/pallas_call | solution.py:20
  (26 shorter events, 1.9 us)
Async XLA Ops:
  0.6 1.0 %copy-start.1 = (s32[4096]{0:T(1024)S(1)}, s32[4096]{0:T(1024)}, u32[]{:S(2)}) copy-start(s32[4096]{0:T(1024)} %param.4) | copy-start | bytes 49156
  0.6 2.3 %collective-permute-start = (f32[32,4096]{1,0:T(8,128)}, f32[32,4096]{1,0:T(8,128)S(1)}, u32[]{:S(2)}, u32[]{:S(2)}) collective-permute-start(f32[32,4096]{1,0:T(8,128)} %slab_ref.1), channel_id=1, source_target_pairs={{0,8},{1,9},{2,10},{3,11},{4,12},{5,13},{6,14},{7,15},{8,0},{9,1},... | collective-permute-start | bytes 1572872 | tf_op jit(solution)/shard_map/ppermute | solution.py:41
  1.2 1.8 %collective-permute-start.1 = (s32[32,128]{1,0:T(8,128)}, s32[32,128]{1,0:T(8,128)S(1)}, u32[]{:S(2)}, u32[]{:S(2)}) collective-permute-start(s32[32,128]{1,0:T(8,128)} %bitcast.4), channel_id=1, source_target_pairs={{0,8},{1,9},{2,10},{3,11},{4,12},{5,13},{6,14},{7,15},{8,0},{9,1},... | collective-permute-start | bytes 49160 | tf_op jit(solution)/shard_map/ppermute | solution.py:41
  1.2 1.7 %collective-permute-start.2 = (s32[1,16]{1,0:T(1,128)}, s32[1,16]{1,0:T(1,128)S(1)}, u32[]{:S(2)}, u32[]{:S(2)}) collective-permute-start(s32[1,16]{1,0:T(1,128)} %bitcast.6), channel_id=1, source_target_pairs={{0,8},{1,9},{2,10},{3,11},{4,12},{5,13},{6,14},{7,15},{8,0},{9,1},... | collective-permute-start | bytes 200 | tf_op jit(solution)/shard_map/ppermute | solution.py:41
  1.7 1.0 %copy-start = (f32[32,4096]{1,0:T(8,128)S(1)}, f32[32,4096]{1,0:T(8,128)}, u32[]{:S(2)}) copy-start(f32[32,4096]{1,0:T(8,128)} %slab_ref.1) | copy-start | bytes 1572868
  3.0 2.9 %copy-start.2 = (s32[16]{0:T(128)S(1)}, s32[16]{0:T(128)}, u32[]{:S(2)}) copy-start(s32[16]{0:T(128)} %param.5) | copy-start | bytes 196
  3.0 7.3 %collective-permute-start.6 = (f32[16,4096]{1,0:T(8,128)S(1)}, f32[16,4096]{1,0:T(8,128)S(1)}, u32[]{:S(2)}, u32[]{:S(2)}) collective-permute-start(f32[16,4096]{1,0:T(8,128)S(1)} %get-tuple-element.18.own_ref), channel_id=1, source_target_pairs={{0,16},{1,17},{2,18},{3,19},{4,20},{5,21},{6,22},{7,23},{8,12},{9,... | collective-permute-start | bytes 786440 | tf_op jit(solution)/shard_map/ppermute | solution.py:41
  6.0 7.5 %collective-permute-start.3 = (f32[16,4096]{1,0:T(8,128)S(1)}, f32[16,4096]{1,0:T(8,128)S(1)}, u32[]{:S(2)}, u32[]{:S(2)}) collective-permute-start(f32[16,4096]{1,0:T(8,128)S(1)} %get-tuple-element.16.own_ref), channel_id=1, source_target_pairs={{0,1},{1,0},{2,3},{3,2},{4,5},{5,4},{6,7},{7,6},{8,10},{9,11},{10,... | collective-permute-start | bytes 786440 | tf_op jit(solution)/shard_map/ppermute | solution.py:41
  10.3 10.6 %collective-permute-start.7 = (f32[16,4224]{1,0:T(8,128)S(1)}, f32[16,4224]{1,0:T(8,128)S(1)}, u32[]{:S(2)}, u32[]{:S(2)}) collective-permute-start(f32[16,4224]{1,0:T(8,128)S(1)} %shard_map.63.own_ref), channel_id=1, source_target_pairs={{0,4},{1,5},{2,6},{3,7},{4,0},{5,1},{6,2},{7,3},{8,24},{9,25},{10,... | collective-permute-start | bytes 811016 | tf_op jit(solution)/shard_map/ppermute | solution.py:41
  13.5 9.4 %collective-permute-start.4 = (f32[16,4224]{1,0:T(8,128)S(1)}, f32[16,4224]{1,0:T(8,128)S(1)}, u32[]{:S(2)}, u32[]{:S(2)}) collective-permute-start(f32[16,4224]{1,0:T(8,128)S(1)} %shard_map.61.own_ref), channel_id=1, source_target_pairs={{0,2},{1,3},{2,0},{3,1},{4,6},{5,7},{6,4},{7,5},{8,9},{9,8},{10,11... | collective-permute-start | bytes 811016 | tf_op jit(solution)/shard_map/ppermute | solution.py:41
  21.0 6.4 %collective-permute-start.8 = (f32[16,4096]{1,0:T(8,128)S(1)}, f32[16,4096]{1,0:T(8,128)S(1)}, u32[]{:S(2)}, u32[]{:S(2)}) collective-permute-start(f32[16,4096]{1,0:T(8,128)S(1)} %shard_map.64.own_ref), channel_id=1, source_target_pairs={{0,1},{1,0},{2,3},{3,2},{4,5},{5,4},{6,7},{7,6},{8,10},{9,11},{10,... | collective-permute-start | bytes 786440 | tf_op jit(solution)/shard_map/ppermute | solution.py:41
  23.0 6.4 %collective-permute-start.5 = (f32[16,4096]{1,0:T(8,128)S(1)}, f32[16,4096]{1,0:T(8,128)S(1)}, u32[]{:S(2)}, u32[]{:S(2)}) collective-permute-start(f32[16,4096]{1,0:T(8,128)S(1)} %shard_map.62.own_ref), channel_id=1, source_target_pairs={{0,16},{1,17},{2,18},{3,19},{4,20},{5,21},{6,22},{7,23},{8,12},{9,... | collective-permute-start | bytes 786440 | tf_op jit(solution)/shard_map/ppermute | solution.py:41
  29.4 10.3 %collective-permute-start.9 = (f32[16,4096]{1,0:T(8,128)S(1)}, f32[16,4096]{1,0:T(8,128)S(1)}, u32[]{:S(2)}, u32[]{:S(2)}) collective-permute-start(f32[16,4096]{1,0:T(8,128)S(1)} %shard_map.66.chunk_ref.own_ref), channel_id=1, source_target_pairs={{0,4},{1,5},{2,6},{3,7},{4,0},{5,1},{6,2},{7,3},{8,24},{9,25},{10,... | collective-permute-start | bytes 786440 | tf_op jit(solution)/shard_map/ppermute | solution.py:41
  31.1 10.8 %collective-permute-start.10 = (f32[16,4096]{1,0:T(8,128)S(1)}, f32[16,4096]{1,0:T(8,128)S(1)}, u32[]{:S(2)}, u32[]{:S(2)}) collective-permute-start(f32[16,4096]{1,0:T(8,128)S(1)} %shard_map.69.own_ref), channel_id=1, source_target_pairs={{0,2},{1,3},{2,0},{3,1},{4,6},{5,7},{6,4},{7,5},{8,9},{9,8},{10,11... | collective-permute-start | bytes 786440 | tf_op jit(solution)/shard_map/ppermute | solution.py:41
  34.6 10.3 %all-to-all-start = ((f32[32,8,128]{2,1,0:T(8,128)}), f32[32,8,128]{2,1,0:T(8,128)S(1)}, u32[]{:S(2)}, u32[]{:S(2)}) async-start(f32[32,8,128]{2,1,0:T(8,128)} %get-tuple-element.25), calls=%async_computation | async-start | bytes 262144 | tf_op jit(solution)/shard_map/all_to_all | solution.py:397
  42.2 1.4 %collective-permute-start.12 = (f32[8,4096]{1,0:T(8,128)S(1)}, f32[8,4096]{1,0:T(8,128)S(1)}, u32[]{:S(2)}, u32[]{:S(2)}) collective-permute-start(f32[8,4096]{1,0:T(8,128)S(1)} %get-tuple-element.23), channel_id=1, source_target_pairs={{0,8},{1,9},{2,10},{3,11},{4,12},{5,13},{6,14},{7,15},{8,0},{9,1},... | collective-permute-start | bytes 393224 | tf_op jit(solution)/shard_map/ppermute | solution.py:41
  42.3 1.5 %collective-permute-start.11 = (f32[8,4096]{1,0:T(8,128)S(1)}, f32[8,4096]{1,0:T(8,128)S(1)}, u32[]{:S(2)}, u32[]{:S(2)}) collective-permute-start(f32[8,4096]{1,0:T(8,128)S(1)} %get-tuple-element.22), channel_id=1, source_target_pairs={{0,8},{1,9},{2,10},{3,11},{4,12},{5,13},{6,14},{7,15},{8,0},{9,1},... | collective-permute-start | bytes 393224 | tf_op jit(solution)/shard_map/ppermute | solution.py:41

commit v5 on v4

--- a/solution.py
+++ b/solution.py
@@ -43,12 +43,6 @@
 
 def chosen_mask(place, core, masks):
     return jnp.where(place & core == 0, masks[0], masks[1])
-
-
-def combine(current, partner, core, masks):
-    place = lax.axis_index(AXES)
-    lower = place & chosen_mask(place, core, masks) == 0
-    return jnp.where(lower, current + partner, partner - current)
 
 
 def three_parts(values):
@@ -138,10 +132,6 @@
     factor = jnp.where(place_ref[0] & chosen_mask(place_ref[0], core, masks) == 0, 1.0, -1.0)
     width = out_ref.shape[1]
     out_ref[...] = own_ref[:, :width] * factor + other_ref[:, :width]
-
-
-def step_after_kernel(core, masks, place_ref, own_ref, other_ref, after_ref, out_ref):
-    step_kernel(core, masks, place_ref, own_ref, other_ref, out_ref)
 
 
 def pick(core, samples, masks, place_ref, tile_ref, chunk_ref, other_ref):
@@ -163,15 +153,12 @@
     return share * jnp.where(own_chip, side, 1.0)
 
 
-def pick_kernel(core, samples, masks, place_ref, tile_ref, chunk_ref, other_ref, out_ref):
-    out_ref[...] = pick(core, samples, masks, place_ref, tile_ref, chunk_ref, other_ref)
-
-
-def pick_all_kernel(core, samples, masks, place_ref, tile_ref, chunk_ref, other_ref, early_ref, out_ref, token_ref):
+def pick_all_kernel(core, samples, masks, place_ref, tile_ref, chunk_ref, other_ref, second_ref, second_other_ref, out_ref, token_ref):
     token_ref[...] = jnp.zeros_like(token_ref)
-    late = pick(core, samples, masks, place_ref, tile_ref, chunk_ref, other_ref)
+    late = pick(core, samples, masks[0], place_ref, tile_ref, chunk_ref, other_ref)
+    early = pick(core, samples, masks[1], place_ref, tile_ref, second_ref, second_other_ref)
     lane = lax.broadcasted_iota(jnp.int32, late.shape, 1)
-    tile = jnp.where(lane < LANES // 2, late, pltpu.roll(early_ref[...], LANES // 2, 1))
+    tile = jnp.where(lane < LANES // 2, late, pltpu.roll(early, LANES // 2, 1))
     for place in range(out_ref.shape[0]):
         out_ref[place] = tile
 
@@ -272,8 +259,9 @@
     shaped = jnp.einsum("cak,az->czk", shaped, table(outer), precision=lax.Precision.HIGHEST)
     current = shaped.reshape(columns, local_rows)
     for bit in range(count.bit_length() - 1):
-        masks = (1 << bit, 1 << bit)
-        current = combine(current, exchange(current, 1, masks), 1, masks)
+        other = exchange(current, 1, (1 << bit, 1 << bit))
+        lower = lax.axis_index(AXES) & 1 << bit == 0
+        current = jnp.where(lower, current + other, other - current)
     sketch = jnp.take(current, sample_offset, axis=1)
     gram = jnp.dot(sketch, sketch.T, precision=lax.Precision.HIGHEST)
     return (current, sketch, lax.psum(gram, AXES) / jnp.float32(samples * count))
@@ -294,8 +282,8 @@
     scaling = 1.0 / math.sqrt(local_rows * count)
     across = (core, core)
     orders = [
-        [(y, z_low), (z_low, y), (x, z_high), (z_high, x)],
-        [(x, z_high), (z_high, x), (y, z_low), (z_low, y)],
+        [(y, z_low), (x, z_high), (z_high, y), (z_low, x)],
+        [(x, z_high), (y, z_low), (z_low, x), (z_high, y)],
     ]
 
     other = exchange(matrix_slab, core, across)
@@ -322,64 +310,45 @@
     )
     ridden, thirds = [], []
     for current, order in zip(chunks, orders):
-        partner = exchange(current, core, order[0])
         current = call(
-            functools.partial(ride_kernel, core, order[0]),
+            functools.partial(step_kernel, core, order[0]),
+            chunk,
+            [IN_SMEM] + [IN_VMEM] * 2,
+            [place, current, exchange(current, core, order[0])],
+        )
+        current = call(
+            functools.partial(ride_kernel, core, order[1]),
             block(2 * ROWS, local_rows + LANES),
             [IN_SMEM] + [IN_VMEM] * 3,
-            [place, current, partner, tile],
-        )
-        partner = exchange(current, core, order[1])
+            [place, current, exchange(current, core, order[1]), tile],
+        )
+        partner = exchange(current, core, order[2])
         ridden.append(partner)
-        current = call(
-            functools.partial(step_kernel, core, order[1]),
-            chunk,
-            [IN_SMEM] + [IN_VMEM] * 2,
-            [place, current, partner],
-        )
-        thirds.append((current, exchange(current, core, order[2])))
+        thirds.append(
+            call(
+                functools.partial(step_kernel, core, order[2]),
+                chunk,
+                [IN_SMEM] + [IN_VMEM] * 2,
+                [place, current, partner],
+            )
+        )
+    first, second = thirds
     last_masks = [order[3] for order in orders]
-    second = combine(*thirds[1], core, orders[1][2])
-    early = call(
-        functools.partial(pick_kernel, core, samples, last_masks[1]),
-        block(ROWS, LANES),
-        [IN_SMEM] + [IN_VMEM] * 3,
-        [place, tile, second, ridden[0]],
-    )
-    first = call(
-        functools.partial(step_after_kernel, core, orders[0][2]),
-        chunk,
-        [IN_SMEM] + [IN_VMEM] * 3,
-        [place, *thirds[0], early],
-    )
     shares, picked = call(
-        functools.partial(pick_all_kernel, core, samples, last_masks[0]),
+        functools.partial(pick_all_kernel, core, samples, last_masks),
         [jax.ShapeDtypeStruct((count, ROWS, LANES), jnp.float32), block(ROWS, LANES)],
-        [IN_SMEM] + [IN_VMEM] * 4,
-        [place, tile, first, ridden[1], early],
-    )
-    later = call(
-        functools.partial(step_after_kernel, core, orders[1][2]),
-        chunk,
-        [IN_SMEM] + [IN_VMEM] * 3,
-        [place, *thirds[1], picked],
+        [IN_SMEM] + [IN_VMEM] * 5,
+        [place, tile, first, ridden[1], second, ridden[0]],
     )
     lasts = [
         call(
-            functools.partial(last_kernel, core, last_masks[0]),
+            functools.partial(last_kernel, core, masks),
             [block(ROWS, local_rows)] * 2,
             [IN_SMEM] + [IN_VMEM] * 3,
-            [place, first, exchange(first, core, last_masks[0]), picked],
-        )
+            [place, current, exchange(current, core, masks), picked],
+        )
+        for current, masks in zip((first, second), last_masks)
     ]
-    lasts.append(
-        call(
-            functools.partial(last_kernel, core, last_masks[1]),
-            [block(ROWS, local_rows)] * 2,
-            [IN_SMEM] + [IN_VMEM] * 3,
-            [place, later, exchange(later, core, last_masks[1]), lasts[0][0]],
-        )
-    )
     kept = [keep for keep, _ in lasts]
     back = [exchange(send, core, across) for _, send in lasts]
     transformed, token = call(

time: 46.1 us -> 45.3 us (0.983)
  starting transfers between devices: 21.1 us -> 19.8 us
  waiting for transfers between devices: 18.9 us -> 19.5 us
    ppermute x13, starting transfers between devices: 18.5 us -> 15.1 us  [exchange(): return lax.ppermute(array, AXES, route)]
    all_to_all x1, waiting for transfers between devices: 0.27 us -> 2.45 us  [local(): lax.all_to_all(shares, AXES, 0, 0, tiled=True)]
    all_to_all x1, starting transfers between devices: 2.56 us -> 4.72 us  [local(): lax.all_to_all(shares, AXES, 0, 0, tiled=True)]
    ppermute x13, waiting for transfers between devices: 18.6 us -> 17 us  [exchange(): return lax.ppermute(array, AXES, route)]
    pallas_call x15 -> x14, Pallas kernels: 4.1 us -> 3.97 us  [call(): pl.pallas_call(body, out_shape=outputs, in_specs=in_specs, out_specs=jax....]
  transfers between devices with their start and end apart: 14 -> 14, of which waited for: 10 -> 9; matrix products, arithmetic and copies ran while one was open for 0% -> 0% of each run, Pallas kernels for 7% -> 6%
where the time goes in v5:
time: 45.3 us; the launch traced here: 45 us
  starting transfers between devices  19.8 us (44%)
  waiting for transfers between devices  19.5 us (43%)
  Pallas kernels  3.97 us (9%)
  local copies, waits for them, and re-layouts  1.05 us (2%)
  between operations  0.74 us (2%)
    ppermute x13, waiting for transfers between devices, exchange(): return lax.ppermute(array, AXES, route)  17 us
    ppermute x13, starting transfers between devices, exchange(): return lax.ppermute(array, AXES, route)  15.1 us
    all_to_all x1, starting transfers between devices, local(): lax.all_to_all(shares, AXES, 0, 0, tiled=True)  4.72 us
    pallas_call x14, Pallas kernels, call(): pl.pallas_call(body, out_shape=outputs, in_specs=in_specs, out_specs=jax....  3.97 us
    all_to_all x1, waiting for transfers between devices, local(): lax.all_to_all(shares, AXES, 0, 0, tiled=True)  2.45 us
    unnamed x6, local copies, waits for them, and re-layouts  1.05 us
  transfers between devices with their start and end apart: 14, of which 9 were waited for; matrix products, arithmetic and copies ran while one was open for 0% of the time, Pallas kernels for 6%

profile of v5, /device:TPU:0, one launch (start us, length us, event | category | flops | bytes accessed | tf_op | source)
XLA Modules:
  0.0 45.0 jit_solution(14393612908213758147)
XLA Ops:
  0.6 0.5 %collective-permute-start = (f32[32,4096]{1,0:T(8,128)}, f32[32,4096]{1,0:T(8,128)S(1)}, u32[]{:S(2)}, u32[]{:S(2)}) collective-permute-start(f32[32,4096]{1,0:T(8,128)} %slab_ref.1), channel_id=1, source_target_pairs={{0,8},{1,9},{2,10},{3,11},{4,12},{5,13},{6,14},{7,15},{8,0},{9,1},... | collective-permute-start | bytes 1572872 | tf_op jit(solution)/shard_map/ppermute | solution.py:41
  1.2 0.4 collective-permute-start.2
  1.7 1.0 %copy-done = f32[32,4096]{1,0:T(8,128)S(1)} copy-done((f32[32,4096]{1,0:T(8,128)S(1)}, f32[32,4096]{1,0:T(8,128)}, u32[]{:S(2)}) %copy-start) | copy-done | bytes 524312
  3.0 2.9 %collective-permute-start.7 = (f32[16,4096]{1,0:T(8,128)S(1)}, f32[16,4096]{1,0:T(8,128)S(1)}, u32[]{:S(2)}, u32[]{:S(2)}) collective-permute-start(f32[16,4096]{1,0:T(8,128)S(1)} %get-tuple-element.18.own_ref), channel_id=1, source_target_pairs={{0,16},{1,17},{2,18},{3,19},{4,20},{5,21},{6,22},{7,23},{8,12},{9,... | collective-permute-start | bytes 786440 | tf_op jit(solution)/shard_map/ppermute | solution.py:41
  5.9 1.5 %collective-permute-start.3 = (f32[16,4096]{1,0:T(8,128)S(1)}, f32[16,4096]{1,0:T(8,128)S(1)}, u32[]{:S(2)}, u32[]{:S(2)}) collective-permute-start(f32[16,4096]{1,0:T(8,128)S(1)} %get-tuple-element.16.own_ref), channel_id=1, source_target_pairs={{0,1},{1,0},{2,3},{3,2},{4,5},{5,4},{6,7},{7,6},{8,10},{9,11},{10,... | collective-permute-start | bytes 786440 | tf_op jit(solution)/shard_map/ppermute | solution.py:41
  7.4 2.8 %collective-permute-done.7.other_ref = f32[16,4096]{1,0:T(8,128)S(1)} collective-permute-done((f32[16,4096]{1,0:T(8,128)S(1)}, f32[16,4096]{1,0:T(8,128)S(1)}, u32[]{:S(2)}, u32[]{:S(2)}) %collective-permute-start.7) | collective-permute-done | bytes 262176 | tf_op jit(solution)/shard_map/ppermute | solution.py:41
  10.3 2.1 %collective-permute-start.8 = (f32[16,4096]{1,0:T(8,128)S(1)}, f32[16,4096]{1,0:T(8,128)S(1)}, u32[]{:S(2)}, u32[]{:S(2)}) collective-permute-start(f32[16,4096]{1,0:T(8,128)S(1)} %shard_map.64.own_ref), channel_id=1, source_target_pairs={{0,1},{1,0},{2,3},{3,2},{4,5},{5,4},{6,7},{7,6},{8,10},{9,11},{10,... | collective-permute-start | bytes 786440 | tf_op jit(solution)/shard_map/ppermute | solution.py:41
  12.5 1.6 %collective-permute-start.4 = (f32[16,4096]{1,0:T(8,128)S(1)}, f32[16,4096]{1,0:T(8,128)S(1)}, u32[]{:S(2)}, u32[]{:S(2)}) collective-permute-start(f32[16,4096]{1,0:T(8,128)S(1)} %shard_map.60.own_ref), channel_id=1, source_target_pairs={{0,16},{1,17},{2,18},{3,19},{4,20},{5,21},{6,22},{7,23},{8,12},{9,... | collective-permute-start | bytes 786440 | tf_op jit(solution)/shard_map/ppermute | solution.py:41
  14.1 2.7 %collective-permute-done.8.other_ref = f32[16,4096]{1,0:T(8,128)S(1)} collective-permute-done((f32[16,4096]{1,0:T(8,128)S(1)}, f32[16,4096]{1,0:T(8,128)S(1)}, u32[]{:S(2)}, u32[]{:S(2)}) %collective-permute-start.8) | collective-permute-done | bytes 262176 | tf_op jit(solution)/shard_map/ppermute | solution.py:41
  16.8 2.1 %collective-permute-start.9 = (f32[16,4224]{1,0:T(8,128)S(1)}, f32[16,4224]{1,0:T(8,128)S(1)}, u32[]{:S(2)}, u32[]{:S(2)}) collective-permute-start(f32[16,4224]{1,0:T(8,128)S(1)} %shard_map.65.own_ref), channel_id=1, source_target_pairs={{0,2},{1,3},{2,0},{3,1},{4,6},{5,7},{6,4},{7,5},{8,24},{9,25},{10,... | collective-permute-start | bytes 811016 | tf_op jit(solution)/shard_map/ppermute | solution.py:41
  19.0 2.7 %collective-permute-start.5 = (f32[16,4224]{1,0:T(8,128)S(1)}, f32[16,4224]{1,0:T(8,128)S(1)}, u32[]{:S(2)}, u32[]{:S(2)}) collective-permute-start(f32[16,4224]{1,0:T(8,128)S(1)} %shard_map.62.own_ref), channel_id=1, source_target_pairs={{0,4},{1,5},{2,6},{3,7},{4,0},{5,1},{6,2},{7,3},{8,9},{9,8},{10,11... | collective-permute-start | bytes 811016 | tf_op jit(solution)/shard_map/ppermute | solution.py:41
  21.7 5.7 %collective-permute-done.9.other_ref = f32[16,4224]{1,0:T(8,128)S(1)} collective-permute-done((f32[16,4224]{1,0:T(8,128)S(1)}, f32[16,4224]{1,0:T(8,128)S(1)}, u32[]{:S(2)}, u32[]{:S(2)}) %collective-permute-start.9) | collective-permute-done | bytes 270368 | tf_op jit(solution)/shard_map/ppermute | solution.py:41
  27.4 0.5 %collective-permute-start.10 = (f32[16,4096]{1,0:T(8,128)S(1)}, f32[16,4096]{1,0:T(8,128)S(1)}, u32[]{:S(2)}, u32[]{:S(2)}) collective-permute-start(f32[16,4096]{1,0:T(8,128)S(1)} %shard_map.66.second_ref.own_ref), channel_id=1, source_target_pairs={{0,4},{1,5},{2,6},{3,7},{4,0},{5,1},{6,2},{7,3},{8,9},{9,8},{10,11... | collective-permute-start | bytes 786440 | tf_op jit(solution)/shard_map/ppermute | solution.py:41
  27.8 2.0 %collective-permute-done.5.other_ref.second_other_ref = f32[16,4224]{1,0:T(8,128)S(1)} collective-permute-done((f32[16,4224]{1,0:T(8,128)S(1)}, f32[16,4224]{1,0:T(8,128)S(1)}, u32[]{:S(2)}, u32[]{:S(2)}) %collective-permute-start.5) | collective-permute-done | bytes 270368 | tf_op jit(solution)/shard_map/ppermute | solution.py:41
  29.9 0.5 %collective-permute-start.6 = (f32[16,4096]{1,0:T(8,128)S(1)}, f32[16,4096]{1,0:T(8,128)S(1)}, u32[]{:S(2)}, u32[]{:S(2)}) collective-permute-start(f32[16,4096]{1,0:T(8,128)S(1)} %shard_map.63.chunk_ref.own_ref), channel_id=1, source_target_pairs={{0,2},{1,3},{2,0},{3,1},{4,6},{5,7},{6,4},{7,5},{8,24},{9,25},{10,... | collective-permute-start | bytes 786440 | tf_op jit(solution)/shard_map/ppermute | solution.py:41
  30.4 1.2 %shard_map.67 = (f32[32,8,128]{2,1,0:T(8,128)}, f32[8,128]{1,0:T(8,128)S(1)}) custom-call(s32[1]{0:T(128)} %bitcast.place_ref, f32[8,128]{1,0:T(8,128)S(1)} %shard_map.61.tile_ref, f32[16,4096]{1,0:T(8,128)S(1)} %shard_map.63.chunk_ref.own_ref, f32[16,4224]{1,0:T(8,128)S(1)} %collective-permute-done.9.other_ref, ...), custom_call_target="tpu_custom_call" | custom-call | tf_op jit(solution)/shard_map/pallas_call | solution.py:20
  31.6 4.7 %all-to-all-start = ((f32[32,8,128]{2,1,0:T(8,128)}), f32[32,8,128]{2,1,0:T(8,128)S(1)}, u32[]{:S(2)}, u32[]{:S(2)}) async-start(f32[32,8,128]{2,1,0:T(8,128)} %get-tuple-element.25), calls=%async_computation | async-start | bytes 262144 | tf_op jit(solution)/shard_map/all_to_all | solution.py:366
  36.3 0.7 %collective-permute-done.10.other_ref = f32[16,4096]{1,0:T(8,128)S(1)} collective-permute-done((f32[16,4096]{1,0:T(8,128)S(1)}, f32[16,4096]{1,0:T(8,128)S(1)}, u32[]{:S(2)}, u32[]{:S(2)}) %collective-permute-start.10) | collective-permute-done | bytes 262176 | tf_op jit(solution)/shard_map/ppermute | solution.py:41
  37.0 0.3 shard_map.69
  37.4 1.6 %collective-permute-done.6.other_ref = f32[16,4096]{1,0:T(8,128)S(1)} collective-permute-done((f32[16,4096]{1,0:T(8,128)S(1)}, f32[16,4096]{1,0:T(8,128)S(1)}, u32[]{:S(2)}, u32[]{:S(2)}) %collective-permute-start.6) | collective-permute-done | bytes 262176 | tf_op jit(solution)/shard_map/ppermute | solution.py:41
  39.4 1.3 %collective-permute-done.11.refs_2_ = f32[8,4096]{1,0:T(8,128)S(1)} collective-permute-done((f32[8,4096]{1,0:T(8,128)S(1)}, f32[8,4096]{1,0:T(8,128)S(1)}, u32[]{:S(2)}, u32[]{:S(2)}) %collective-permute-start.11) | collective-permute-done | bytes 131104 | tf_op jit(solution)/shard_map/ppermute | solution.py:41
  40.8 0.8 %shard_map.70 = (f32[32,4096]{1,0:T(8,128)}, f32[8,128]{1,0:T(8,128)S(1)}) custom-call(s32[1]{0:T(128)} %bitcast.place_ref, f32[8,4096]{1,0:T(8,128)S(1)} %get-tuple-element.20.refs_0_, f32[8,4096]{1,0:T(8,128)S(1)} %get-tuple-element.21.refs_1_, f32[8,4096]{1,0:T(8,128)S(1)} %collective-permute-done.11.refs_2_, f32[8,4096]{1,0:T(8,128)S(1)} %collective-permute-done.12.refs_3_), custom_call_target="tpu_custom_call" | custom-call | tf_op jit(solution)/shard_map/pallas_call | solution.py:20
  41.6 2.4 %all-to-all-done.shares_ref = f32[32,8,128]{2,1,0:T(8,128)S(1)} async-done(((f32[32,8,128]{2,1,0:T(8,128)}), f32[32,8,128]{2,1,0:T(8,128)S(1)}, u32[]{:S(2)}, u32[]{:S(2)}) %all-to-all-start) | async-done | bytes 131104 | tf_op jit(solution)/shard_map/all_to_all | solution.py:366
  44.0 1.0 %shard_map.71 = (f32[32,32]{1,0:T(8,128)}, f32[16,32]{1,0:T(8,128)}) custom-call(s32[1]{0:T(128)} %bitcast.place_ref, f32[32,8,128]{2,1,0:T(8,128)S(1)} %all-to-all-done.shares_ref, f32[8,128]{1,0:T(8,128)S(1)} %get-tuple-element.26.after_ref), custom_call_target="tpu_custom_call" | custom-call | tf_op jit(solution)/shard_map/pallas_call | solution.py:20
  (24 shorter events, 1.1 us)
Async XLA Ops:
  0.6 1.0 %copy-start.1 = (s32[4096]{0:T(1024)S(1)}, s32[4096]{0:T(1024)}, u32[]{:S(2)}) copy-start(s32[4096]{0:T(1024)} %param.4) | copy-start | bytes 49156
  0.6 2.3 %collective-permute-start = (f32[32,4096]{1,0:T(8,128)}, f32[32,4096]{1,0:T(8,128)S(1)}, u32[]{:S(2)}, u32[]{:S(2)}) collective-permute-start(f32[32,4096]{1,0:T(8,128)} %slab_ref.1), channel_id=1, source_target_pairs={{0,8},{1,9},{2,10},{3,11},{4,12},{5,13},{6,14},{7,15},{8,0},{9,1},... | collective-permute-start | bytes 1572872 | tf_op jit(solution)/shard_map/ppermute | solution.py:41
  1.2 1.8 %collective-permute-start.1 = (s32[32,128]{1,0:T(8,128)}, s32[32,128]{1,0:T(8,128)S(1)}, u32[]{:S(2)}, u32[]{:S(2)}) collective-permute-start(s32[32,128]{1,0:T(8,128)} %bitcast.4), channel_id=1, source_target_pairs={{0,8},{1,9},{2,10},{3,11},{4,12},{5,13},{6,14},{7,15},{8,0},{9,1},... | collective-permute-start | bytes 49160 | tf_op jit(solution)/shard_map/ppermute | solution.py:41
  1.2 1.7 %collective-permute-start.2 = (s32[1,16]{1,0:T(1,128)}, s32[1,16]{1,0:T(1,128)S(1)}, u32[]{:S(2)}, u32[]{:S(2)}) collective-permute-start(s32[1,16]{1,0:T(1,128)} %bitcast.6), channel_id=1, source_target_pairs={{0,8},{1,9},{2,10},{3,11},{4,12},{5,13},{6,14},{7,15},{8,0},{9,1},... | collective-permute-start | bytes 200 | tf_op jit(solution)/shard_map/ppermute | solution.py:41
  1.7 1.0 %copy-start = (f32[32,4096]{1,0:T(8,128)S(1)}, f32[32,4096]{1,0:T(8,128)}, u32[]{:S(2)}) copy-start(f32[32,4096]{1,0:T(8,128)} %slab_ref.1) | copy-start | bytes 1572868
  3.0 7.3 %collective-permute-start.7 = (f32[16,4096]{1,0:T(8,128)S(1)}, f32[16,4096]{1,0:T(8,128)S(1)}, u32[]{:S(2)}, u32[]{:S(2)}) collective-permute-start(f32[16,4096]{1,0:T(8,128)S(1)} %get-tuple-element.18.own_ref), channel_id=1, source_target_pairs={{0,16},{1,17},{2,18},{3,19},{4,20},{5,21},{6,22},{7,23},{8,12},{9,... | collective-permute-start | bytes 786440 | tf_op jit(solution)/shard_map/ppermute | solution.py:41
  5.9 6.5 %collective-permute-start.3 = (f32[16,4096]{1,0:T(8,128)S(1)}, f32[16,4096]{1,0:T(8,128)S(1)}, u32[]{:S(2)}, u32[]{:S(2)}) collective-permute-start(f32[16,4096]{1,0:T(8,128)S(1)} %get-tuple-element.16.own_ref), channel_id=1, source_target_pairs={{0,1},{1,0},{2,3},{3,2},{4,5},{5,4},{6,7},{7,6},{8,10},{9,11},{10,... | collective-permute-start | bytes 786440 | tf_op jit(solution)/shard_map/ppermute | solution.py:41
  10.3 6.5 %collective-permute-start.8 = (f32[16,4096]{1,0:T(8,128)S(1)}, f32[16,4096]{1,0:T(8,128)S(1)}, u32[]{:S(2)}, u32[]{:S(2)}) collective-permute-start(f32[16,4096]{1,0:T(8,128)S(1)} %shard_map.64.own_ref), channel_id=1, source_target_pairs={{0,1},{1,0},{2,3},{3,2},{4,5},{5,4},{6,7},{7,6},{8,10},{9,11},{10,... | collective-permute-start | bytes 786440 | tf_op jit(solution)/shard_map/ppermute | solution.py:41
  12.5 1.6 %copy-start.2 = (s32[16]{0:T(128)S(1)}, s32[16]{0:T(128)}, u32[]{:S(2)}) copy-start(s32[16]{0:T(128)} %param.5) | copy-start | bytes 196
  12.5 6.5 %collective-permute-start.4 = (f32[16,4096]{1,0:T(8,128)S(1)}, f32[16,4096]{1,0:T(8,128)S(1)}, u32[]{:S(2)}, u32[]{:S(2)}) collective-permute-start(f32[16,4096]{1,0:T(8,128)S(1)} %shard_map.60.own_ref), channel_id=1, source_target_pairs={{0,16},{1,17},{2,18},{3,19},{4,20},{5,21},{6,22},{7,23},{8,12},{9,... | collective-permute-start | bytes 786440 | tf_op jit(solution)/shard_map/ppermute | solution.py:41
  16.8 10.5 %collective-permute-start.9 = (f32[16,4224]{1,0:T(8,128)S(1)}, f32[16,4224]{1,0:T(8,128)S(1)}, u32[]{:S(2)}, u32[]{:S(2)}) collective-permute-start(f32[16,4224]{1,0:T(8,128)S(1)} %shard_map.65.own_ref), channel_id=1, source_target_pairs={{0,2},{1,3},{2,0},{3,1},{4,6},{5,7},{6,4},{7,5},{8,24},{9,25},{10,... | collective-permute-start | bytes 811016 | tf_op jit(solution)/shard_map/ppermute | solution.py:41
  19.0 10.8 %collective-permute-start.5 = (f32[16,4224]{1,0:T(8,128)S(1)}, f32[16,4224]{1,0:T(8,128)S(1)}, u32[]{:S(2)}, u32[]{:S(2)}) collective-permute-start(f32[16,4224]{1,0:T(8,128)S(1)} %shard_map.62.own_ref), channel_id=1, source_target_pairs={{0,4},{1,5},{2,6},{3,7},{4,0},{5,1},{6,2},{7,3},{8,9},{9,8},{10,11... | collective-permute-start | bytes 811016 | tf_op jit(solution)/shard_map/ppermute | solution.py:41
  27.4 9.7 %collective-permute-start.10 = (f32[16,4096]{1,0:T(8,128)S(1)}, f32[16,4096]{1,0:T(8,128)S(1)}, u32[]{:S(2)}, u32[]{:S(2)}) collective-permute-start(f32[16,4096]{1,0:T(8,128)S(1)} %shard_map.66.second_ref.own_ref), channel_id=1, source_target_pairs={{0,4},{1,5},{2,6},{3,7},{4,0},{5,1},{6,2},{7,3},{8,9},{9,8},{10,11... | collective-permute-start | bytes 786440 | tf_op jit(solution)/shard_map/ppermute | solution.py:41
  29.9 9.1 %collective-permute-start.6 = (f32[16,4096]{1,0:T(8,128)S(1)}, f32[16,4096]{1,0:T(8,128)S(1)}, u32[]{:S(2)}, u32[]{:S(2)}) collective-permute-start(f32[16,4096]{1,0:T(8,128)S(1)} %shard_map.63.chunk_ref.own_ref), channel_id=1, source_target_pairs={{0,2},{1,3},{2,0},{3,1},{4,6},{5,7},{6,4},{7,5},{8,24},{9,25},{10,... | collective-permute-start | bytes 786440 | tf_op jit(solution)/shard_map/ppermute | solution.py:41
  31.6 12.5 %all-to-all-start = ((f32[32,8,128]{2,1,0:T(8,128)}), f32[32,8,128]{2,1,0:T(8,128)S(1)}, u32[]{:S(2)}, u32[]{:S(2)}) async-start(f32[32,8,128]{2,1,0:T(8,128)} %get-tuple-element.25), calls=%async_computation | async-start | bytes 262144 | tf_op jit(solution)/shard_map/all_to_all | solution.py:366
  37.3 2.1 %collective-permute-start.12 = (f32[8,4096]{1,0:T(8,128)S(1)}, f32[8,4096]{1,0:T(8,128)S(1)}, u32[]{:S(2)}, u32[]{:S(2)}) collective-permute-start(f32[8,4096]{1,0:T(8,128)S(1)} %get-tuple-element.23), channel_id=1, source_target_pairs={{0,8},{1,9},{2,10},{3,11},{4,12},{5,13},{6,14},{7,15},{8,0},{9,1},... | collective-permute-start | bytes 393224 | tf_op jit(solution)/shard_map/ppermute | solution.py:41
  39.3 1.4 %collective-permute-start.11 = (f32[8,4096]{1,0:T(8,128)S(1)}, f32[8,4096]{1,0:T(8,128)S(1)}, u32[]{:S(2)}, u32[]{:S(2)}) collective-permute-start(f32[8,4096]{1,0:T(8,128)S(1)} %get-tuple-element.22), channel_id=1, source_target_pairs={{0,8},{1,9},{2,10},{3,11},{4,12},{5,13},{6,14},{7,15},{8,0},{9,1},... | collective-permute-start | bytes 393224 | tf_op jit(solution)/shard_map/ppermute | solution.py:41
